TPU v7x, 512 devices: a whole 4x8x8 slice. The times are simulated.
512 devices in a mesh: dp: 16 (over x, y_lo, core), owner: 32 (over y_hi, z).
Axes of the slice: x: 4, y: 8 (y_hi: 4, y_lo: 2; y = y_hi * 2 + y_lo), z: 8, core: 2. Of those that a mesh axis runs over, the one named last changes fastest.
Arguments:
- train_act: bfloat16 [2048, 4096], P('dp', 'owner')
- train_grad: bfloat16 [2048, 10240], P('dp', 'owner')
- query_act: bfloat16 [16, 4096], P(None, 'owner'), may hold values from -6 to 6
- query_grad: bfloat16 [16, 10240], P(None, 'owner'), may hold values from -6 to 6
- query_of: int32 [16], replicated, may hold values from 0 to 7, as said below
- counts: int32 [16], replicated, may hold values from 1 to 128, 1536 in all
- eig_act: bfloat16 [4096, 4096], P(None, 'owner')
- eig_grad: bfloat16 [10240, 10240], P('dp', 'owner')
Outputs:
- scores: float32 [8, 2048], P(None, ('dp', 'owner'))
- corrections: float32 [4096, 10240], P('dp', 'owner')
Inputs may be any that keep to these rules, and one draw needn't show every extreme that they name: `query_of`: each of the 8 queries owns exactly 2 rows.
All inputs are finite; a program needn't handle non-finite values.
Results may differ from a plain program's by a relative error of at most 0.019.
Values may be sent and summed in bfloat16 or wider, within the bound.
A program may use at most 64 MiB of HBM per device.

v0:
```python
import math

import jax
import jax.numpy as jnp
from jax import lax
from jax.sharding import PartitionSpec as P

D = 4096
FF = 10240
QUERIES = 8
QTOK = 2


damping = 0.1


def per_device(train_act, train_grad, query_act, query_grad, query_of, counts, eig_act, eig_grad):
    tok_rows = train_act.shape[0]
    stacked_act = jnp.concatenate([train_act, query_act], 0)
    stacked_grad = jnp.concatenate([train_grad, query_grad], 0)
    full_act, full_grad = (
        lax.all_gather(stacked_act, "owner", axis=1, tiled=True),
        lax.all_gather(stacked_grad, "owner", axis=1, tiled=True),
    )
    rotated_grad = jnp.dot(
        full_grad,
        lax.all_gather(eig_grad, "dp", axis=0, tiled=True),
        preferred_element_type=jnp.float32,
    ).astype(jnp.bfloat16)
    part_act = jnp.dot(full_act, eig_act, preferred_element_type=jnp.float32).astype(jnp.bfloat16)
    rotated_act = lax.all_gather(part_act, "owner", axis=1, tiled=True)
    train_ra = rotated_act[:tok_rows]
    query_ra = rotated_act[tok_rows:]
    train_rg = rotated_grad[:tok_rows]
    query_rg = rotated_grad[tok_rows:]
    dp_count = lax.axis_size("dp")
    dp_index = lax.axis_index("dp")
    shard_ids = jnp.arange(dp_count, dtype=jnp.int32)
    own_count = jnp.sum(jnp.where(shard_ids == dp_index, counts, 0))
    valid = (jnp.arange(tok_rows, dtype=jnp.int32) < own_count).astype(jnp.float32)
    total_count = jnp.sum(counts).astype(jnp.float32)
    squares_act = (train_ra.astype(jnp.float32) ** 2 * valid[:, None]).astype(jnp.bfloat16)
    squares_grad = (train_rg.astype(jnp.float32) ** 2).astype(jnp.bfloat16)
    grouped = jnp.argsort(query_of, stable=True).reshape(QUERIES, QTOK)
    factor = 1.0 / math.sqrt(D * FF * QTOK)
    share_rows = train_ra.shape[1] // dp_count

    def weights(members, correction, act_source):
        act_sel = act_source[members].astype(jnp.float32)
        grad_sel = query_rg[members].astype(jnp.float32)
        products = jnp.sum(act_sel[:, :, None] * grad_sel[:, None, :], axis=0)
        return (products / correction).astype(jnp.bfloat16)

    partial_value = lax.dot_general(
        squares_act, squares_grad, (((0,), (0,)), ((), ())), preferred_element_type=jnp.float32
    )
    summed = lax.psum(partial_value.astype(jnp.bfloat16), "dp").astype(jnp.float32)
    correction = summed / total_count + damping

    def score_local(members):
        weighted = weights(members, correction, query_ra)
        mixed_rows = jnp.dot(train_ra, weighted, preferred_element_type=jnp.float32)
        return jnp.sum(mixed_rows * train_rg.astype(jnp.float32), axis=1) * valid * factor

    local_scores = lax.map(score_local, grouped)
    owned_out = lax.dynamic_slice_in_dim(correction, dp_index * share_rows, share_rows, 0)
    return (lax.psum_scatter(local_scores, "owner", scatter_dimension=1, tiled=True), owned_out)


def solution(mesh):
    in_specs = (
        P("dp", "owner"),
        P("dp", "owner"),
        P(None, "owner"),
        P(None, "owner"),
        P(),
        P(),
        P(None, "owner"),
        P("dp", "owner"),
    )
    out_specs = (P(None, ("dp", "owner")), P("dp", "owner"))
    return jax.shard_map(
        per_device, mesh=mesh, in_specs=in_specs, out_specs=out_specs, check_vma=False
    )
```

profile of v0, /device:TPU:32, one launch (start us, length us, event | category | flops | bytes accessed | tf_op | source)
XLA Modules:
  0.0 674.6 jit_solution(12087344012512851620)
XLA Ops:
  7.2 1.5 pad_maximum_fusion
  8.8 1.0 copy.27
  9.8 1.4 maximum_bitcast_fusion
  11.2 0.7 all-gather.10.cloned.1.call-update
  11.9 81.3 %all-gather.6.cloned.1.call-done = bf16[144,4096]{1,0:T(8,128)(2,1)} async-done(((bf16[144,128]{1,0:T(8,128)(2,1)}), bf16[144,4096]{1,0:T(8,128)(2,1)}) %all-gather.6.cloned.1.call-update) | async-done | bytes 1179664 | tf_op jit(solution)/shard_map/all_gather | solution.py:22
  93.2 2.3 convolution_convert_fusion.2
  95.6 1.4 fusion.13
  97.6 92.5 %all-gather.12.cloned.1.call-done = bf16[32,320,144]{1,2,0:T(8,128)(2,1)} async-done(((bf16[1,320,144]{1,2,0:T(8,128)(2,1)}), bf16[32,320,144]{1,2,0:T(8,128)(2,1)}) %all-gather.12.cloned.1.call-update) | async-done | bytes 2949136 | tf_op jit(solution)/shard_map/all_gather | solution.py:23
  190.1 4.6 copy.28
  194.8 7.1 %reshape.81 = bf16[10240,144]{0,1:T(8,128)(2,1)} reshape(bf16[32,320,144]{1,0,2:T(8,128)(2,1)} %copy.28) | data formatting | bytes 5898240
  201.8 37.2 %all-gather.10.cloned.1.call-done = bf16[10240,320]{0,1:T(8,128)(2,1)} async-done(((bf16[640,320]{0,1:T(8,128)(2,1)}), bf16[10240,320]{0,1:T(8,128)(2,1)}) %all-gather.10.cloned.1.call-update) | async-done | bytes 6553616 | tf_op jit(solution)/shard_map/all_gather | solution.py:27
  239.1 6.2 convolution_convert_fusion.1
  245.3 75.5 %all-gather.8.cloned.1.call-done = bf16[144,4096]{1,0:T(8,128)(2,1)} async-done(((bf16[144,128]{1,0:T(8,128)(2,1)}), bf16[144,4096]{1,0:T(8,128)(2,1)}) %all-gather.8.cloned.1.call-update) | async-done | bytes 1179664 | tf_op jit(solution)/shard_map/all_gather | solution.py:31
  320.8 3.8 convolution_convert_fusion
  325.3 1.2 sort.17
  326.6 1.3 dynamic-slice
  328.9 132.0 %all-reduce.3.cloned.1.call-done = bf16[4096,320]{0,1:T(8,128)(2,1)} async-done(((bf16[4096,320]{0,1:T(8,128)(2,1)}), bf16[4096,320]{0,1:T(8,128)(2,1)}) %all-reduce.3.cloned.1.call-update) | async-done | bytes 2621456 | tf_op jit(solution)/shard_map/psum | solution.py:57
  461.0 4.8 divide_add_fusion
  465.8 43.0 %while.11 = (s32[]{:T(128)}, f32[8,128]{1,0:T(8,128)S(1)}, s32[8,2]{1,0:T(8,128)S(1)}, bf16[16,4096]{1,0:T(8,128)(2,1)S(1)}, bf16[16,320]{1,0:T(8,128)(2,1)S(1)}...) while((s32[]{:T(128)}, f32[8,128]{1,0:T(8,128)S(1)}, ...), condition=%wide.region_7.8_spmd.clone, body=%wide.region_4.7_spmd.clone.sunk | while | flops 342230912 | bytes 37961148 | solution.py:65
  467.0 1.2 multiply_reduce_fusion.2
  468.2 1.2 copy-done.1
  469.4 1.0 fusion.25
  472.4 1.2 multiply_reduce_fusion.2
  473.6 1.2 copy-done.1
  474.8 1.0 fusion.25
  477.7 1.2 multiply_reduce_fusion.2
  479.0 1.2 copy-done.1
  480.2 1.0 fusion.25
  481.2 0.6 fusion.26
  483.1 1.2 multiply_reduce_fusion.2
  484.4 1.2 copy-done.1
  485.6 1.0 fusion.25
  488.5 1.2 multiply_reduce_fusion.2
  489.7 1.2 copy-done.1
  491.0 1.0 fusion.25
  492.0 0.6 fusion.26
  493.9 1.2 multiply_reduce_fusion.2
  495.1 1.2 copy-done.1
  496.3 1.0 fusion.25
  499.2 1.2 multiply_reduce_fusion.2
  500.5 1.2 copy-done.1
  501.7 1.0 fusion.25
  502.7 0.6 fusion.26
  504.6 1.2 multiply_reduce_fusion.2
  505.9 1.2 copy-done.1
  507.1 1.0 fusion.25
  508.9 156.9 %all-reduce = f32[8,128]{0,1:T(8,128)S(1)} all-reduce(f32[8,128]{0,1:T(8,128)S(1)} %copy.30), channel_id=2, replica_groups=mesh['dp'=16,'owner'=32] {'owner'}, use_global_device_ids=true, to_apply=%region_8.9.clone | all-reduce | flops 1024 | bytes 8192
  665.8 1.7 constant_dynamic-slice_fusion.1
  (99 shorter events, 14.8 us)
Async XLA Ops:
  7.2 86.0 %copy-start = (bf16[4096,128]{1,0:T(8,128)(2,1)S(1)}, bf16[4096,128]{1,0:T(8,128)(2,1)}, u32[]{:S(2)}) copy-start(bf16[4096,128]{1,0:T(8,128)(2,1)} %param.16) | copy-start | bytes 3145732
  7.2 86.0 %all-gather.6.cloned.1.call-start = ((), (), s32[]{:S(2)}) async-start(), calls=%async_computation | async-start | bytes 1216512 | tf_op jit(solution)/shard_map/all_gather | solution.py:22
  8.7 181.4 %all-gather.12.cloned.1.call-start = ((), (), s32[]{:S(2)}) async-start(), calls=%async_computation.4 | async-start | bytes 3649536 | tf_op jit(solution)/shard_map/all_gather | solution.py:23
  11.2 227.9 %all-gather.10.cloned.1.call-start = ((), (), s32[]{:S(2)}) async-start(), calls=%async_computation.2 | async-start | bytes 6963200 | tf_op jit(solution)/shard_map/all_gather | solution.py:27
  11.9 308.9 %all-gather.8.cloned.1.call-start = ((), (), s32[]{:S(2)}) async-start(), calls=%async_computation.1 | async-start | bytes 1216512 | tf_op jit(solution)/shard_map/all_gather | solution.py:31
  95.6 365.4 %all-reduce.3.cloned.1.call-start = ((), (), s32[]{:S(2)}) async-start(), calls=%async_computation.3 | async-start | bytes 5242880 | tf_op jit(solution)/shard_map/psum | solution.py:57
  245.3 83.5 %copy-start.3 = (bf16[144,320]{1,0:T(8,128)(2,1)}, bf16[144,320]{1,0:T(8,128)(2,1)S(1)}, u32[]{:S(2)}) copy-start(bf16[144,320]{1,0:T(8,128)(2,1)S(1)} %convolution_convert_fusion.1) | copy-start | bytes 276484
  245.3 80.0 %copy-start.4 = (s32[16]{0:T(128)S(1)}, s32[16]{0:T(128)}, u32[]{:S(2)}) copy-start(s32[16]{0:T(128)} %param.14) | copy-start | bytes 196
  320.8 7.8 %copy-start.2 = (bf16[144,4096]{1,0:T(8,128)(2,1)S(1)}, bf16[144,4096]{1,0:T(8,128)(2,1)}, u32[]{:S(2)}) copy-start(bf16[144,4096]{1,0:T(8,128)(2,1)} %all-gather.8.cloned.1.call-done) | copy-start | bytes 3538948
  328.9 136.9 %slice-start = ((bf16[144,4096]{1,0:T(8,128)(2,1)}), bf16[16,4096]{1,0:T(8,128)(2,1)S(1)}, s32[]{:S(2)}) async-start(bf16[144,4096]{1,0:T(8,128)(2,1)} %all-gather.8.cloned.1.call-done), calls=%async_computation.5 | async-start | bytes 262144 | tf_op jit(solution)/shard_map/slice | solution.py:33
  328.9 136.8 %slice-start.1 = ((bf16[144,320]{1,0:T(8,128)(2,1)}), bf16[16,320]{1,0:T(8,128)(2,1)S(1)}, s32[]{:S(2)}) async-start(bf16[144,320]{1,0:T(8,128)(2,1)} %copy-done.3), calls=%async_computation.6 | async-start | bytes 24576 | tf_op jit(solution)/shard_map/slice | solution.py:35
  467.0 2.5 copy-start.1
  472.3 2.5 copy-start.1
  477.7 2.5 copy-start.1
  483.1 2.5 copy-start.1
  488.5 2.5 copy-start.1
  493.8 2.5 copy-start.1
  499.2 2.5 copy-start.1
  504.6 2.5 copy-start.1
Sparse Core Ops, SparseCore 0:
  11.1 82.0 all-gather.5
  96.9 93.1 all-gather.11
  192.2 46.7 all-gather.9
  242.0 78.8 all-gather.7
  324.7 136.2 all-reduce.2
where the time goes:
time: 676 us; the launch traced here: 675 us
  waiting for transfers between devices  419 us (62%)
  blocking collectives  157 us (23%)
  local copies, waits for them, and re-layouts  36 us (5%)
  other arithmetic  26.2 us (4%)
  matrix products  20.3 us (3%)
  between operations  15.3 us (2%)
    unnamed x1, blocking collectives  157 us
    psum x1, waiting for transfers between devices, per_device(): lax.psum(partial_value.astype(jnp.bfloat16), 'dp').astype(jnp.float32)  132 us
    all_gather x1, waiting for transfers between devices, per_device(): lax.all_gather(stacked_grad, 'owner', axis=1, tiled=True)  92.5 us
    all_gather x1, waiting for transfers between devices, per_device(): lax.all_gather(stacked_act, 'owner', axis=1, tiled=True)  81.3 us
    all_gather x1, waiting for transfers between devices, per_device(): rotated_act = lax.all_gather(part_act, 'owner', axis=1, tiled=True)  75.5 us
    all_gather x1, waiting for transfers between devices, per_device(): lax.all_gather(eig_grad, 'dp', axis=0, tiled=True)  37.2 us
  transfers between devices with their start and end apart: 5, of which 5 were waited for; matrix products, arithmetic and copies ran while one was open for 4% of the time, Pallas kernels for 0%

commit v1 on v0

v1 whole, which is shorter than its diff:
```python
import functools
import math

import jax
import jax.numpy as jnp
from jax import lax
from jax.experimental import pallas as pl
from jax.experimental.pallas import tpu as pltpu
from jax.sharding import PartitionSpec as P

D = 4096
FF = 10240
QUERIES = 8
QTOK = 2
damping = 0.1

MESH = pl.DeviceIdType.MESH
BF = jnp.bfloat16
F32 = jnp.float32

TOK = 128
AC = 128
GC = 320
QR = 16
AR = TOK + QR


def mod(value, size):
    return lax.rem(value + size, size)


def device(x, l, k, h, z):
    return (x * 4 + l * 2 + k, h * 8 + z)


def kernel(ta, tg, qa, qg, qof, cnt, ea, eg, sc_out, corr_out,
           blk_a, act, ea2, ebuf, ss1, qmsg, qb, sbuf, sq, acc, pb, rsb, qpb, rgb, rg,
           rab, rs1, ra, raq, wts, fsc, f1, f2, f3, *sems):
    (a_s, a_r, ar_s, ar_r, e_s, e_r, s0_s, s0_r, s1_s, s1_r, s2_s, s2_r,
     sr_s, sr_r, sq_s, sq_r, rs_s, rs_r, rq_s, rq_r, ag_s, ag_r, fw_s, fw_r,
     r0_s, r0_r, r1_s, r1_r, r2_s, r2_r, rr_s, rr_r, rk_s, rk_r,
     f1_s, f1_r, f2_s, f2_r, f3_s, f3_r, loc) = sems
    dp, owner = lax.axis_index("dp"), lax.axis_index("owner")
    x, l, k = dp // 4, (dp // 2) % 2, dp % 2
    h, z = owner // 8, owner % 8
    za, zr = z // 4, z % 4
    swap = za != l
    partner = device(x, za, k, h, 4 * l + zr)
    chip = l * 4 + x
    shard = chip * 2 + k
    zp, zm = mod(z + 1, 8), mod(z - 1, 8)
    core = device(x, l, 1 - k, h, z)
    up, down = device(x, l, k, h, zp), device(x, l, k, h, zm)

    pending = []

    def copy(src, dst, ss, rs, to):
        return pltpu.make_async_remote_copy(
            src_ref=src, dst_ref=dst, send_sem=ss, recv_sem=rs, device_id=to, device_id_type=MESH)

    def send(src, dst, ss, rs, to, when=None):
        c = copy(src, dst, ss, rs, to)
        if when is None:
            c.start()
        else:
            pl.when(when)(lambda: c.start())
        pending.append((c, when))

    def arrived(dst, rs, when=None):
        c = copy(dst, dst, rs, rs, core)
        if when is None:
            c.wait_recv()
        else:
            pl.when(when)(lambda: c.wait_recv())

    bar = pltpu.get_barrier_semaphore()
    peers = [device(x, l, k, mod(h + j, 4), z) for j in range(1, 4)]
    peers += [device(x, l, k, h, mod(z + j, 8)) for j in range(1, 8)]

    def plane(s):
        return device((s // 2) % 4, s // 8, s % 2, h, z)

    peers += [plane(mod(shard + j, 16)) for j in range(1, 16)]
    for p in peers:
        pl.semaphore_signal(bar, inc=1, device_id=p, device_id_type=MESH)

    @pl.when(swap)
    def _():
        pl.semaphore_signal(bar, inc=1, device_id=partner, device_id_type=MESH)
    blk_a[0:TOK, :] = ta[...]
    blk_a[TOK:AR, :] = qa[...]
    qmsg[...] = jnp.zeros_like(qmsg)
    qmsg[:, 0:GC] = qg[...]

    @pl.when(swap)
    def _():
        pl.semaphore_wait(bar, len(peers) + 1)

    @pl.when(jnp.logical_not(swap))
    def _():
        pl.semaphore_wait(bar, len(peers))

    def act_slot(pos, lo=0, n=4):
        return act.at[:, pl.ds(pl.multiple_of(pos * 512 + lo * 128, 128), n * 128)]

    def act_one(pos, hh):
        return act.at[:, pl.ds(pl.multiple_of(pos * 512 + hh * 128, 128), 128)]

    for j in range(1, 4):
        send(blk_a, act_one(z, h), a_s.at[j], a_r.at[j], device(x, l, k, mod(h + j, 4), z))
    own_act = pltpu.make_async_copy(blk_a, act_one(z, h), loc.at[0])
    own_act.start()

    send(tg, ss1.at[h], s0_s.at[0], s0_r.at[0], partner, swap)
    send(qmsg, qb, s0_s.at[1], s0_r.at[1], partner, swap)
    send(eg, ebuf.at[k], e_s, e_r, core)

    @pl.when(jnp.logical_not(swap))
    def _():
        ss1[h] = tg[...]
        qb[...] = qmsg[...]
    ebuf[k] = eg[...]
    for zz in range(8):
        for hh in range(4):
            ea2[pl.ds(zz * 512 + hh * 128, 128), :] = ea[pl.ds(hh * 1024 + zz * 128, 128), :]

    own_act.wait()
    for j in range(1, 4):
        arrived(act_one(z, mod(h - j, 4)), a_r.at[j])

    def act_ring(hop):
        n = 4 if hop < 4 else 2
        pos = mod(z - hop + 1, 8)
        send(act_slot(pos, 0, n), act_slot(pos, 0, n), ar_s.at[0, hop - 1], ar_r.at[0, hop - 1], up)
        pos = mod(z + hop - 1, 8)
        lo = 4 - n
        send(act_slot(pos, lo, n), act_slot(pos, lo, n), ar_s.at[1, hop - 1], ar_r.at[1, hop - 1], down)

    def act_got(hop):
        n = 4 if hop < 4 else 2
        arrived(act_slot(mod(z - hop, 8), 0, n), ar_r.at[0, hop - 1])
        arrived(act_slot(mod(z + hop, 8), 4 - n, n), ar_r.at[1, hop - 1])

    def act_dot(pos):
        return jnp.dot(act[:, pl.ds(pl.multiple_of(pos * 512, 512), 512)],
                       ea2[pl.ds(pl.multiple_of(pos * 512, 512), 512), :],
                       preferred_element_type=F32)

    act_ring(1)
    arrived(ss1.at[h], s0_r.at[0], swap)
    arrived(qb, s0_r.at[1], swap)
    for j in range(1, 4):
        to = device(x, l, k, mod(h + j, 4), z)
        send(ss1.at[h], ss1.at[h], s1_s.at[j], s1_r.at[j], to)
        send(qb, sq.at[zr], s1_s.at[3 + j], s1_r.at[0], to, h == x)
    total = act_dot(z)
    act_got(1)
    act_ring(2)
    total += act_dot(mod(z - 1, 8)) + act_dot(mod(z + 1, 8))

    for j in range(1, 4):
        hh = mod(h - j, 4)
        arrived(ss1.at[hh], s1_r.at[j])

    def s_slot(pos, half=None, xx=None):
        if xx is not None:
            lanes = pl.ds(pl.multiple_of(xx * 128, 128), 128)
        else:
            lanes = pl.ds(half * 256, 256)
        return sbuf.at[pos // 4, pl.ds(pl.multiple_of((pos % 4) * GC, GC), GC), lanes]

    for j in range(1, 4):
        xt = mod(x + j, 4)
        send(ss1.at[xt], s_slot(z, xx=x), s2_s.at[j], s2_r.at[j], device(xt, l, k, h, z))
    own_s = pltpu.make_async_copy(ss1.at[x], s_slot(z, xx=x), loc.at[1])
    own_s.start()

    @pl.when(h == x)
    def _():
        sq[zr] = qb[...]
    arrived(sq.at[zr], s1_r.at[0], h != x)

    act_got(2)
    act_ring(3)
    total += act_dot(mod(z - 2, 8)) + act_dot(mod(z + 2, 8))

    own_s.wait()
    for j in range(1, 4):
        arrived(s_slot(z, xx=mod(x - j, 4)), s2_r.at[j])

    def s_ring(half, hop):
        if hop < 4 or half == 0:
            pos = mod(z - hop + 1, 8)
            send(s_slot(pos, half), s_slot(pos, half), sr_s.at[0, half, hop - 1], sr_r.at[0, half, hop - 1], up)
        if hop < 4 or half == 1:
            pos = mod(z + hop - 1, 8)
            send(s_slot(pos, half), s_slot(pos, half), sr_s.at[1, half, hop - 1], sr_r.at[1, half, hop - 1], down)

    def s_got(half, hop):
        if hop < 4 or half == 0:
            arrived(s_slot(mod(z - hop, 8), half), sr_r.at[0, half, hop - 1])
        if hop < 4 or half == 1:
            arrived(s_slot(mod(z + hop, 8), half), sr_r.at[1, half, hop - 1])

    s_ring(0, 1)
    s_ring(1, 1)
    send(sq.at[zr], sq.at[zr], sq_s.at[0], sq_r.at[0], up)
    send(sq.at[zr], sq.at[zr], sq_s.at[1], sq_r.at[1], down)

    act_got(3)
    act_ring(4)
    total += act_dot(mod(z - 3, 8)) + act_dot(mod(z + 3, 8))
    acc[...] = jnp.zeros_like(acc)
    arrived(ebuf.at[1 - k], e_r)
    act_got(4)
    total += act_dot(mod(z + 4, 8))
    rab[...] = total.astype(BF)

    send(rab, rs1.at[h], r0_s, r0_r, partner, swap)

    @pl.when(jnp.logical_not(swap))
    def _():
        rs1[h] = rab[...]

    pair = z // 2
    step = 2 * (z % 2) - 1
    order = [pair, mod(pair + step, 4), mod(pair - step, 4), mod(pair + 2, 4)]

    def s_dot(g, half):
        la, m = g // 2, g % 2
        acc[la, :, half * 256:half * 256 + 256] += jnp.dot(
            ebuf[m], sbuf[la, pl.ds(pl.multiple_of(m * 640, 640), 640), half * 256:half * 256 + 256],
            preferred_element_type=F32)

    s_got(0, 1)
    s_ring(0, 2)
    s_got(1, 1)
    s_ring(1, 2)
    arrived(sq.at[mod(zr - 1, 4)], sq_r.at[0])
    arrived(sq.at[mod(zr + 1, 4)], sq_r.at[1])
    send(sq.at[mod(zr - 1, 4)], sq.at[mod(zr - 1, 4)], sq_s.at[2], sq_r.at[2], up)
    s_dot(order[0], 0)
    s_dot(order[0], 1)

    arrived(rs1.at[h], r0_r, swap)
    for j in range(1, 4):
        send(rs1.at[h], rs1.at[h], r1_s.at[j], r1_r.at[j], device(x, l, k, mod(h + j, 4), z))

    s_got(0, 2)
    s_ring(0, 3)
    s_got(1, 2)
    s_ring(1, 3)
    s_dot(order[1], 0)
    s_dot(order[1], 1)

    for j in range(1, 4):
        arrived(rs1.at[mod(h - j, 4)], r1_r.at[j])
    kt = zr // 2
    mine = k == kt

    def ra_block(pos, xx, kk):
        return ra.at[pos // 4, pl.ds(pl.multiple_of(xx * 256 + kk * 128, 128), 128),
                     pl.ds(pl.multiple_of((pos % 2) * 128, 128), 128)]

    def ra_slot(pos, half):
        return ra.at[pos // 4, pl.ds(half * 512, 512), pl.ds(pl.multiple_of((pos % 2) * 128, 128), 128)]

    for j in range(1, 4):
        xt = mod(x + j, 4)
        send(rs1.at[xt, pl.ds(0, TOK), :], ra_block(z, x, k), r2_s.at[j], r2_r.at[j], device(xt, l, k, h, z), mine)
    for j in range(4):
        xt = mod(x + j, 4)
        send(rs1.at[xt, pl.ds(0, TOK), :], ra_block(z, x, k), r2_s.at[4 + j], r2_r.at[4 + j],
             device(xt, l, 1 - k, h, z), jnp.logical_not(mine))

    def raq_slot(pos):
        return raq.at[:, pl.ds(pl.multiple_of((pos % 2) * 128, 128), 128)]

    @pl.when(mine)
    def _():
        a = pltpu.make_async_copy(rs1.at[x, pl.ds(0, TOK), :], ra_block(z, x, k), loc.at[2])
        b = pltpu.make_async_copy(rs1.at[x, pl.ds(TOK, QR), :], raq_slot(z), loc.at[3])
        a.start()
        b.start()
        a.wait()
        b.wait()

    s_got(0, 3)
    s_ring(0, 4)
    s_got(1, 3)
    s_ring(1, 4)
    s_dot(order[2], 0)
    s_dot(order[2], 1)

    for j in range(1, 4):
        arrived(ra_block(z, mod(x - j, 4), k), r2_r.at[j], mine)
    for j in range(4):
        arrived(ra_block(z, mod(x - j, 4), 1 - k), r2_r.at[4 + j], mine)

    def held(pos):
        return (pos % 4) // 2 == k

    def r_ring(hop):
        for half in range(2):
            if hop < 4 or half == 0:
                pos = mod(z - hop + 1, 8)
                send(ra_slot(pos, half), ra_slot(pos, half), rr_s.at[0, half, hop - 1], rr_r.at[0, half, hop - 1],
                     up, held(pos))
            if hop < 4 or half == 1:
                pos = mod(z + hop - 1, 8)
                send(ra_slot(pos, half), ra_slot(pos, half), rr_s.at[1, half, hop - 1], rr_r.at[1, half, hop - 1],
                     down, held(pos))

    def r_got(hop):
        for half in range(2):
            if hop < 4 or half == 0:
                pos = mod(z - hop, 8)
                arrived(ra_slot(pos, half), rr_r.at[0, half, hop - 1], held(pos))
            if hop < 4 or half == 1:
                pos = mod(z + hop, 8)
                arrived(ra_slot(pos, half), rr_r.at[1, half, hop - 1], held(pos))

    r_ring(1)
    send(raq_slot(z), raq_slot(z), rk_s.at[0], rk_r.at[0], up, held(z))
    send(raq_slot(z), raq_slot(z), rk_s.at[1], rk_r.at[1], down, held(z))

    s_got(0, 4)
    s_got(1, 4)
    s_dot(order[3], 0)
    s_dot(order[3], 1)
    for b in range(8):
        pb[b] = acc[b // 4, :, (b % 4) * 128:(b % 4) * 128 + 128].astype(BF)
        send(pb.at[b], rsb.at[chip], rs_s.at[b], rs_r.at[chip], device(b % 4, b // 4, k, h, z), chip != b)

    arrived(sq.at[mod(zr - 2, 4)], sq_r.at[2])
    qpart = jnp.zeros((QR, GC), F32)
    for m in range(2):
        zero = jnp.zeros((QR, 384), F32)
        first = jnp.concatenate([sq[2 * m].astype(F32), zero], axis=1)
        second = jnp.concatenate([sq[2 * m + 1].astype(F32), zero], axis=1)
        both = (first + pltpu.roll(second, GC, 1))[:, 0:640].astype(BF)
        qpart += lax.dot_general(both, ebuf[m], (((1,), (1,)), ((), ())), preferred_element_type=F32)
    qpb[chip] = jnp.concatenate([qpart, jnp.zeros((QR, 64), F32)], axis=1)
    for b in range(8):
        send(qpb.at[chip], qpb.at[chip], rq_s.at[b], rq_r.at[chip], device(b % 4, b // 4, k, h, z), chip != b)

    r_got(1)
    r_ring(2)
    pos = mod(z - 1, 8)
    arrived(raq_slot(pos), rk_r.at[0], held(pos))
    send(raq_slot(pos), raq_slot(pos), rk_s.at[2], rk_r.at[2], up, held(pos))
    pos = mod(z + 1, 8)
    arrived(raq_slot(pos), rk_r.at[1], held(pos))

    rsb[chip] = pb[chip]
    for b in range(8):
        arrived(rsb.at[b], rs_r.at[b], chip != b)
    block = rsb[0].astype(F32)
    for b in range(1, 8):
        block += rsb[b].astype(F32)
    rgb[...] = block.astype(BF)

    def rg_slot(s):
        return rg.at[:, pl.ds(pl.multiple_of(s * 128, 128), 128)]

    for b in range(8):
        send(rgb, rg_slot(shard), ag_s.at[b], ag_r.at[chip], device(b % 4, b // 4, k, h, z), chip != b)
    send(rgb, rg_slot(shard), fw_s.at[chip], fw_r.at[chip], core)
    own_rg = pltpu.make_async_copy(rgb, rg_slot(shard), loc.at[4])
    own_rg.start()

    r_got(2)
    r_ring(3)
    for b in range(8):
        arrived(rg_slot(2 * b + k), ag_r.at[b], chip != b)
        send(rg_slot(2 * b + k), rg_slot(2 * b + k), fw_s.at[b], fw_r.at[b], core, chip != b)
    r_got(3)
    r_ring(4)
    pos = mod(z - 2, 8)
    arrived(raq_slot(pos), rk_r.at[2], held(pos))
    own_rg.wait()
    for b in range(8):
        arrived(rg_slot(2 * b + 1 - k), fw_r.at[b])
    r_got(4)

    tokens = 0
    for s in range(16):
        tokens = tokens + cnt[s]
    tokens = tokens.astype(F32)
    corr_out[...] = jnp.zeros_like(corr_out)
    row = lax.broadcasted_iota(jnp.int32, (256, 1), 0)

    for c in range(8):
        s = (c % 4) * 4 + (c // 4) * 2
        limit = jnp.where(row < 128, cnt[s], cnt[s + 1] + 128)
        ok = (row < limit).astype(F32)
        a = ra[c // 4, (c % 4) * 256:(c % 4) * 256 + 256, :].astype(F32)
        g = rg[:, c * 256:c * 256 + 256].astype(F32)
        corr_out[...] += jnp.dot((g * g).astype(BF), (a * a * ok).astype(BF), preferred_element_type=F32)
    corr = corr_out[...] / tokens + damping
    corr_out[...] = corr

    for b in range(8):
        arrived(qpb.at[b], rq_r.at[b], chip != b)
    qsum = qpb[0]
    for b in range(1, 8):
        qsum += qpb[b]
    qrows = qsum.astype(BF).astype(F32)
    lane = lax.broadcasted_iota(jnp.int32, (QR, 384), 0)
    of = jnp.zeros((QR, 384), jnp.int32)
    for s in range(QR):
        of = jnp.where(lane == s, qof[s], of)
    for q in range(QUERIES):
        picked = jnp.where(of == q, qrows, 0.0).T.astype(BF)[0:GC, :]
        prod = jnp.dot(picked, raq[...], preferred_element_type=F32)
        wts[q] = (prod / corr_out[...]).astype(BF)

    def chunk(c, carry):
        rac = ra[c // 4, pl.ds(pl.multiple_of((c % 4) * 256, 256), 256), :]
        rgc = rg[:, pl.ds(pl.multiple_of(c * 256, 256), 256)].astype(F32)
        rows = []
        for q in range(QUERIES):
            mixed = lax.dot_general(wts[q], rac, (((1,), (1,)), ((), ())), preferred_element_type=F32)
            rows.append(jnp.sum(mixed * rgc, axis=0, keepdims=True))
        fsc[:, pl.ds(pl.multiple_of(c * 256, 256), 256)] = jnp.concatenate(rows, axis=0)
        return carry

    lax.fori_loop(0, 8, chunk, 0)

    for s in range(16):
        send(fsc.at[:, pl.ds(s * 128, 128)], f1.at[shard], f1_s.at[s], f1_r.at[shard],
             device((s // 2) % 4, s // 8, s % 2, h, z), shard != s)
    f1[shard] = fsc[:, pl.ds(pl.multiple_of(shard * 128, 128), 128)]
    for s in range(16):
        arrived(f1.at[s], f1_r.at[s], shard != s)
    part = f1[0]
    for s in range(1, 16):
        part += f1[s]
    f2[h] = part
    for j in range(1, 4):
        send(f2.at[h], f2.at[h], f2_s.at[j], f2_r.at[j], device(x, l, k, mod(h + j, 4), z))
    for j in range(1, 4):
        arrived(f2.at[mod(h - j, 4)], f2_r.at[j])
    f3[z] = f2[0] + f2[1] + f2[2] + f2[3]
    for j in range(1, 8):
        send(f3.at[z], f3.at[z], f3_s.at[j], f3_r.at[j], device(x, l, k, h, mod(z + j, 8)))
    for j in range(1, 8):
        arrived(f3.at[mod(z - j, 8)], f3_r.at[j])
    done = f3[0]
    for j in range(1, 8):
        done += f3[j]
    t = lax.broadcasted_iota(jnp.int32, (8, 128), 1)
    done = jnp.where(t < cnt[dp], done, 0.0) * (1.0 / math.sqrt(D * FF * QTOK))
    sc_out[...] = pltpu.roll(done, mod(128 - 4 * owner, 128), 1)

    for c, when in pending:
        if when is None:
            c.wait_send()
        else:
            pl.when(when)(functools.partial(lambda c: c.wait_send(), c))


def per_device(train_act, train_grad, query_act, query_grad, query_of, counts, eig_act, eig_grad):
    vm = pl.BlockSpec(memory_space=pltpu.VMEM)
    sm = pl.BlockSpec(memory_space=pltpu.SMEM)
    V = pltpu.VMEM
    dma = pltpu.SemaphoreType.DMA
    scratch = [
        V((AR, AC), BF), V((AR, D), BF), V((D, AC), BF), V((2, GC, 640), BF),
        V((4, GC, TOK), BF), V((QR, 384), BF), V((QR, 384), BF), V((2, 1280, 512), BF), V((4, QR, 384), BF),
        V((2, GC, 512), F32), V((8, GC, TOK), BF), V((8, GC, TOK), BF), V((8, QR, 384), F32),
        V((GC, TOK), BF), V((GC, 2048), BF),
        V((AR, AC), BF), V((4, AR, AC), BF), V((2, 1024, 256), BF), V((QR, 256), BF),
        V((QUERIES, GC, 256), BF), V((8, 2048), F32), V((16, 8, 128), F32), V((4, 8, 128), F32), V((8, 8, 128), F32),
    ]
    counts_of = [
        (4,), (4,), (2, 4), (2, 4), (), (), (2,), (2,), (7,), (4,), (4,), (4,),
        (2, 2, 4), (2, 2, 4), (3,), (3,), (8,), (8,), (8,), (8,), (8,), (8,), (8,), (8,),
        (), (), (4,), (4,), (8,), (8,), (2, 2, 4), (2, 2, 4), (3,), (3,),
        (16,), (16,), (4,), (4,), (8,), (8,), (5,),
    ]
    scratch += [dma(n) if n else dma for n in counts_of]
    scores, corr = pl.pallas_call(
        kernel,
        out_shape=(jax.ShapeDtypeStruct((8, 128), F32), jax.ShapeDtypeStruct((GC, 256), F32)),
        in_specs=[vm, vm, vm, vm, sm, sm, vm, vm],
        out_specs=(vm, vm),
        scratch_shapes=scratch,
        compiler_params=pltpu.CompilerParams(
            collective_id=0, has_side_effects=True, vmem_limit_bytes=48 * 2**20),
    )(train_act, train_grad.T, query_act, query_grad, query_of, counts, eig_act, eig_grad.T)
    return scores[:, :4], corr.T


def solution(mesh):
    in_specs = (
        P("dp", "owner"),
        P("dp", "owner"),
        P(None, "owner"),
        P(None, "owner"),
        P(),
        P(),
        P(None, "owner"),
        P("dp", "owner"),
    )
    out_specs = (P(None, ("dp", "owner")), P("dp", "owner"))
    return jax.shard_map(
        per_device, mesh=mesh, in_specs=in_specs, out_specs=out_specs, check_vma=False
    )
```

time: 676 us -> 123 us (0.18)
  the two profiles are of different devices: /device:TPU:32 before, /device:TPU:16 now
where the time goes in v1:
time: 123 us
  Pallas kernels  115 us (93%)
  local copies, waits for them, and re-layouts  7.29 us (6%)
    pallas_call x1, Pallas kernels, per_device(): pl.pallas_call(kernel, out_shape=(jax.ShapeDtypeStruct((8, 128), F32), ja...  115 us
    unnamed x18, local copies, waits for them, and re-layouts  7.29 us

profile of v1, /device:TPU:16, one launch (start us, length us, event | category | flops | bytes accessed | tf_op | source)
XLA Modules:
  0.0 123.1 jit_solution(14646970677446271299)
XLA Ops:
  0.6 0.0 copy-start.6
  0.6 0.0 copy-start.7
  0.7 0.6 copy-done.6
  1.3 0.0 copy-done.7
  1.3 0.0 copy-start
  1.3 1.2 copy-done
  2.5 0.0 copy-start.1
  2.5 1.0 copy-done.1
  3.5 0.0 copy-start.2
  3.5 0.9 copy-done.2
  4.4 0.0 copy-start.3
  4.4 0.8 copy-done.3
  5.2 0.0 copy-start.4
  5.2 0.7 copy-done.4
  5.9 0.0 copy-start.5
  5.9 0.7 copy-done.5
  6.6 115.1 %shard_map.95 = (f32[8,128]{1,0:T(8,128)S(1)}, f32[320,256]{1,0:T(8,128)S(1)}) custom-call(bf16[128,128]{1,0:T(8,128)(2,1)S(1)} %copy-done.3, bf16[320,128]{1,0:T(8,128)(2,1)S(1)} %bitcast.6, bf16[16,128]{1,0:T(8,128)(2,1)S(1)} %copy-done.5, bf16[16,320]{1,0:T(8,128)(2,1)S(1)} %copy-done.4, s32[16]{0:T(128)S(1)} %copy-done.6, s32[16]{0:T(128)S(1)} %copy-done.7, ...), custom_call_target="tpu_custom_call" | custom-call | tf_op jit(solution)/shard_map/pallas_call | solution.py:483
  121.7 0.7 copy.10
  122.4 0.7 copy.12
Async XLA Ops:
  0.6 0.7 copy-start.6
  0.6 0.7 copy-start.7
  1.3 1.2 copy-start
  2.5 1.0 copy-start.1
  3.5 0.9 copy-start.2
  4.4 0.8 copy-start.3
  5.2 0.7 copy-start.4
  5.9 0.7 copy-start.5

commit v2 on v1

--- a/solution.py
+++ b/solution.py
@@ -33,11 +33,11 @@
     return (x * 4 + l * 2 + k, h * 8 + z)
 
 
-def kernel(ta, tg, qa, qg, qof, cnt, ea, eg, sc_out, corr_out,
-           blk_a, act, ea2, ebuf, ss1, qmsg, qb, sbuf, sq, acc, pb, rsb, qpb, rgb, rg,
+def kernel(ta, tg, qa, qg, qof_in, cnt_in, ea, eg, sc_out, corr_out,
+           qof, cnt, qgv, tgv, ld, blk_a, act, ea2, ebuf, qmsg, gbuf, sq, acc, qpb, rgb, rg,
            rab, rs1, ra, raq, wts, fsc, f1, f2, f3, *sems):
-    (a_s, a_r, ar_s, ar_r, e_s, e_r, s0_s, s0_r, s1_s, s1_r, s2_s, s2_r,
-     sr_s, sr_r, sq_s, sq_r, rs_s, rs_r, rq_s, rq_r, ag_s, ag_r, fw_s, fw_r,
+    (a_s, a_r, ar_s, ar_r, ec_s, ec_r, ex_s, ex_r, s1_s, s1_r,
+     sr_s, sr_r, sq_s, sq_r, rq_s, rq_r, ag_s, ag_r, fw_s, fw_r,
      r0_s, r0_r, r1_s, r1_r, r2_s, r2_r, rr_s, rr_r, rk_s, rk_r,
      f1_s, f1_r, f2_s, f2_r, f3_s, f3_r, loc) = sems
     dp, owner = lax.axis_index("dp"), lax.axis_index("owner")
@@ -87,10 +87,20 @@
     @pl.when(swap)
     def _():
         pl.semaphore_signal(bar, inc=1, device_id=partner, device_id_type=MESH)
-    blk_a[0:TOK, :] = ta[...]
-    blk_a[TOK:AR, :] = qa[...]
+
+    def local(src, dst, sem):
+        c = pltpu.make_async_copy(src, dst, sem)
+        c.start()
+        return c
+
+    loads = [local(ta, blk_a.at[pl.ds(0, TOK), :], ld.at[0]), local(qa, blk_a.at[pl.ds(TOK, QR), :], ld.at[1]),
+             local(qg, qgv, ld.at[2]), local(tg, tgv, ld.at[3]), local(eg, ebuf.at[dp], ld.at[4]),
+             local(qof_in, qof, ld.at[5]), local(cnt_in, cnt, ld.at[6])]
+    loads += [local(ea.at[hh], ea2.at[:, hh], ld.at[7 + hh]) for hh in range(4)]
+    for c in loads:
+        c.wait()
     qmsg[...] = jnp.zeros_like(qmsg)
-    qmsg[:, 0:GC] = qg[...]
+    qmsg[:, 0:GC] = qgv[...]
 
     @pl.when(swap)
     def _():
@@ -108,21 +118,43 @@
 
     for j in range(1, 4):
         send(blk_a, act_one(z, h), a_s.at[j], a_r.at[j], device(x, l, k, mod(h + j, 4), z))
-    own_act = pltpu.make_async_copy(blk_a, act_one(z, h), loc.at[0])
-    own_act.start()
-
-    send(tg, ss1.at[h], s0_s.at[0], s0_r.at[0], partner, swap)
-    send(qmsg, qb, s0_s.at[1], s0_r.at[1], partner, swap)
-    send(eg, ebuf.at[k], e_s, e_r, core)
-
-    @pl.when(jnp.logical_not(swap))
+    own_act = local(blk_a, act_one(z, h), loc.at[0])
+
+    def g_one(pos, hh):
+        return gbuf.at[hh, pl.ds(pl.multiple_of(pos * GC, GC), GC), :]
+
+    def g_slot(pos, half):
+        return gbuf.at[pl.ds(half * 2, 2), pl.ds(pl.multiple_of(pos * GC, GC), GC), :]
+
+    for j in range(1, 4):
+        send(tgv, g_one(z, h), s1_s.at[j], s1_r.at[j], device(x, l, k, mod(h + j, 4), z))
+    own_g = local(tgv, g_one(z, h), loc.at[1])
+
+    for j in range(1, 4):
+        send(qmsg, sq.at[zr], sq_s.at[j], sq_r.at[7], device(x, l, k, mod(h + j, 4), z),
+             jnp.logical_and(h == x, za == l))
+
+    @pl.when(jnp.logical_and(h == x, za == l))
     def _():
-        ss1[h] = tg[...]
-        qb[...] = qmsg[...]
-    ebuf[k] = eg[...]
-    for zz in range(8):
-        for hh in range(4):
-            ea2[pl.ds(zz * 512 + hh * 128, 128), :] = ea[pl.ds(hh * 1024 + zz * 128, 128), :]
+        sq[zr] = qmsg[...]
+
+    def e_at(xx, ll, part=None):
+        d = xx * 4 + ll * 2 + k
+        if part is None:
+            return ebuf.at[d]
+        return ebuf.at[d, pl.ds(part * 160, 160), :]
+
+    xp, xm, xo = mod(x + 1, 4), mod(x - 1, 4), mod(x + 2, 4)
+    right, left = device(xp, l, k, h, z), device(xm, l, k, h, z)
+    beside = device(x, 1 - l, k, h, z)
+
+    def e_pass(xx, ll, i):
+        send(e_at(xx, ll), e_at(xx, ll), ec_s.at[i], ec_r.at[i], core)
+
+    send(e_at(x, l), e_at(x, l), ex_s.at[0], ex_r.at[0], beside)
+    send(e_at(x, l), e_at(x, l), ex_s.at[1], ex_r.at[1], right)
+    send(e_at(x, l), e_at(x, l), ex_s.at[2], ex_r.at[2], left)
+    e_pass(x, l, 0)
 
     own_act.wait()
     for j in range(1, 4):
@@ -143,104 +175,76 @@
 
     def act_dot(pos):
         return jnp.dot(act[:, pl.ds(pl.multiple_of(pos * 512, 512), 512)],
-                       ea2[pl.ds(pl.multiple_of(pos * 512, 512), 512), :],
+                       ea2[pos].reshape(512, 128),
                        preferred_element_type=F32)
 
+    def s_ring(half, hop):
+        if hop < 4 or half == 0:
+            pos = mod(z - hop + 1, 8)
+            send(g_slot(pos, half), g_slot(pos, half), sr_s.at[0, half, hop - 1], sr_r.at[0, half, hop - 1], up)
+        if hop < 4 or half == 1:
+            pos = mod(z + hop - 1, 8)
+            send(g_slot(pos, half), g_slot(pos, half), sr_s.at[1, half, hop - 1], sr_r.at[1, half, hop - 1], down)
+
+    def s_got(half, hop):
+        if hop < 4 or half == 0:
+            arrived(g_slot(mod(z - hop, 8), half), sr_r.at[0, half, hop - 1])
+        if hop < 4 or half == 1:
+            arrived(g_slot(mod(z + hop, 8), half), sr_r.at[1, half, hop - 1])
+
     act_ring(1)
-    arrived(ss1.at[h], s0_r.at[0], swap)
-    arrived(qb, s0_r.at[1], swap)
-    for j in range(1, 4):
-        to = device(x, l, k, mod(h + j, 4), z)
-        send(ss1.at[h], ss1.at[h], s1_s.at[j], s1_r.at[j], to)
-        send(qb, sq.at[zr], s1_s.at[3 + j], s1_r.at[0], to, h == x)
     total = act_dot(z)
+    own_g.wait()
+    for j in range(1, 4):
+        arrived(g_one(z, mod(h - j, 4)), s1_r.at[j])
+    s_ring(0, 1)
+    s_ring(1, 1)
+    arrived(sq.at[zr], sq_r.at[7], jnp.logical_and(h != x, za == l))
+    for j in range(1, 8):
+        send(sq.at[zr], sq.at[zr], sq_s.at[3 + j], sq_r.at[j - 1],
+             device(x, l, k, h, mod(z + j, 8)), za == l)
     act_got(1)
     act_ring(2)
     total += act_dot(mod(z - 1, 8)) + act_dot(mod(z + 1, 8))
 
-    for j in range(1, 4):
-        hh = mod(h - j, 4)
-        arrived(ss1.at[hh], s1_r.at[j])
-
-    def s_slot(pos, half=None, xx=None):
-        if xx is not None:
-            lanes = pl.ds(pl.multiple_of(xx * 128, 128), 128)
-        else:
-            lanes = pl.ds(half * 256, 256)
-        return sbuf.at[pos // 4, pl.ds(pl.multiple_of((pos % 4) * GC, GC), GC), lanes]
-
-    for j in range(1, 4):
-        xt = mod(x + j, 4)
-        send(ss1.at[xt], s_slot(z, xx=x), s2_s.at[j], s2_r.at[j], device(xt, l, k, h, z))
-    own_s = pltpu.make_async_copy(ss1.at[x], s_slot(z, xx=x), loc.at[1])
-    own_s.start()
-
-    @pl.when(h == x)
-    def _():
-        sq[zr] = qb[...]
-    arrived(sq.at[zr], s1_r.at[0], h != x)
-
+    arrived(e_at(x, 1 - l), ex_r.at[0])
+    send(e_at(x, 1 - l), e_at(x, 1 - l), ex_s.at[3], ex_r.at[3], right)
+    send(e_at(x, 1 - l), e_at(x, 1 - l), ex_s.at[4], ex_r.at[4], left)
+    e_pass(x, 1 - l, 1)
     act_got(2)
     act_ring(3)
     total += act_dot(mod(z - 2, 8)) + act_dot(mod(z + 2, 8))
 
-    own_s.wait()
-    for j in range(1, 4):
-        arrived(s_slot(z, xx=mod(x - j, 4)), s2_r.at[j])
-
-    def s_ring(half, hop):
-        if hop < 4 or half == 0:
-            pos = mod(z - hop + 1, 8)
-            send(s_slot(pos, half), s_slot(pos, half), sr_s.at[0, half, hop - 1], sr_r.at[0, half, hop - 1], up)
-        if hop < 4 or half == 1:
-            pos = mod(z + hop - 1, 8)
-            send(s_slot(pos, half), s_slot(pos, half), sr_s.at[1, half, hop - 1], sr_r.at[1, half, hop - 1], down)
-
-    def s_got(half, hop):
-        if hop < 4 or half == 0:
-            arrived(s_slot(mod(z - hop, 8), half), sr_r.at[0, half, hop - 1])
-        if hop < 4 or half == 1:
-            arrived(s_slot(mod(z + hop, 8), half), sr_r.at[1, half, hop - 1])
-
-    s_ring(0, 1)
-    s_ring(1, 1)
-    send(sq.at[zr], sq.at[zr], sq_s.at[0], sq_r.at[0], up)
-    send(sq.at[zr], sq.at[zr], sq_s.at[1], sq_r.at[1], down)
+    arrived(e_at(xm, l), ex_r.at[1])
+    send(e_at(xm, l, 0), e_at(xm, l, 0), ex_s.at[5], ex_r.at[5], right)
+    e_pass(xm, l, 2)
+    arrived(e_at(xp, l), ex_r.at[2])
+    send(e_at(xp, l, 1), e_at(xp, l, 1), ex_s.at[6], ex_r.at[6], left)
+    e_pass(xp, l, 3)
 
     act_got(3)
     act_ring(4)
     total += act_dot(mod(z - 3, 8)) + act_dot(mod(z + 3, 8))
-    acc[...] = jnp.zeros_like(acc)
-    arrived(ebuf.at[1 - k], e_r)
-    act_got(4)
-    total += act_dot(mod(z + 4, 8))
-    rab[...] = total.astype(BF)
-
-    send(rab, rs1.at[h], r0_s, r0_r, partner, swap)
-
-    @pl.when(jnp.logical_not(swap))
-    def _():
-        rs1[h] = rab[...]
-
-    pair = z // 2
-    step = 2 * (z % 2) - 1
-    order = [pair, mod(pair + step, 4), mod(pair - step, 4), mod(pair + 2, 4)]
-
-    def s_dot(g, half):
-        la, m = g // 2, g % 2
-        acc[la, :, half * 256:half * 256 + 256] += jnp.dot(
-            ebuf[m], sbuf[la, pl.ds(pl.multiple_of(m * 640, 640), 640), half * 256:half * 256 + 256],
-            preferred_element_type=F32)
-
     s_got(0, 1)
     s_ring(0, 2)
     s_got(1, 1)
     s_ring(1, 2)
-    arrived(sq.at[mod(zr - 1, 4)], sq_r.at[0])
-    arrived(sq.at[mod(zr + 1, 4)], sq_r.at[1])
-    send(sq.at[mod(zr - 1, 4)], sq.at[mod(zr - 1, 4)], sq_s.at[2], sq_r.at[2], up)
-    s_dot(order[0], 0)
-    s_dot(order[0], 1)
+    act_got(4)
+    total += act_dot(mod(z + 4, 8))
+    rab[...] = total.astype(BF)
+
+    send(rab, rs1.at[h], r0_s, r0_r, partner, swap)
+
+    @pl.when(jnp.logical_not(swap))
+    def _():
+        rs1[h] = rab[...]
+
+    arrived(e_at(xm, 1 - l), ex_r.at[3])
+    send(e_at(xm, 1 - l, 0), e_at(xm, 1 - l, 0), ex_s.at[7], ex_r.at[7], right)
+    e_pass(xm, 1 - l, 4)
+    arrived(e_at(xp, 1 - l), ex_r.at[4])
+    send(e_at(xp, 1 - l, 1), e_at(xp, 1 - l, 1), ex_s.at[8], ex_r.at[8], left)
+    e_pass(xp, 1 - l, 5)
 
     arrived(rs1.at[h], r0_r, swap)
     for j in range(1, 4):
@@ -250,8 +254,6 @@
     s_ring(0, 3)
     s_got(1, 2)
     s_ring(1, 3)
-    s_dot(order[1], 0)
-    s_dot(order[1], 1)
 
     for j in range(1, 4):
         arrived(rs1.at[mod(h - j, 4)], r1_r.at[j])
@@ -285,12 +287,17 @@
         a.wait()
         b.wait()
 
+    arrived(e_at(xo, l, 0), ex_r.at[5])
+    arrived(e_at(xo, l, 1), ex_r.at[6])
+    e_pass(xo, l, 6)
+    arrived(e_at(xo, 1 - l, 0), ex_r.at[7])
+    arrived(e_at(xo, 1 - l, 1), ex_r.at[8])
+    e_pass(xo, 1 - l, 7)
+
     s_got(0, 3)
     s_ring(0, 4)
     s_got(1, 3)
     s_ring(1, 4)
-    s_dot(order[2], 0)
-    s_dot(order[2], 1)
 
     for j in range(1, 4):
         arrived(ra_block(z, mod(x - j, 4), k), r2_r.at[j], mine)
@@ -324,25 +331,49 @@
     send(raq_slot(z), raq_slot(z), rk_s.at[0], rk_r.at[0], up, held(z))
     send(raq_slot(z), raq_slot(z), rk_s.at[1], rk_r.at[1], down, held(z))
 
-    s_got(0, 4)
-    s_got(1, 4)
-    s_dot(order[3], 0)
-    s_dot(order[3], 1)
-    for b in range(8):
-        pb[b] = acc[b // 4, :, (b % 4) * 128:(b % 4) * 128 + 128].astype(BF)
-        send(pb.at[b], rsb.at[chip], rs_s.at[b], rs_r.at[chip], device(b % 4, b // 4, k, h, z), chip != b)
-
-    arrived(sq.at[mod(zr - 2, 4)], sq_r.at[2])
+    e_of = [(x, l), (x, 1 - l), (xm, l), (xp, l), (xm, 1 - l), (xp, 1 - l), (xo, l), (xo, 1 - l)]
+    for i, (xx, ll) in enumerate(e_of):
+        arrived(ebuf.at[xx * 4 + ll * 2 + 1 - k], ec_r.at[i])
+    pair = z // 2
+    step = 2 * (z % 2) - 1
+    order = [pair, mod(pair + step, 4), mod(pair - step, 4), mod(pair + 2, 4)]
+
+    def s_dot(n):
+        out = jnp.zeros((GC, TOK), F32)
+        for hh in range(4):
+            out += jnp.dot(ebuf[hh * 4 + n], gbuf[hh, pl.ds(pl.multiple_of(n * 640, 640), 640), :],
+                           preferred_element_type=F32)
+        return out
+
+    acc[...] = s_dot(order[0]) + s_dot(order[1])
+    acc[...] += s_dot(order[2])
+
+    for j in range(1, 8):
+        from_z = mod(z - j, 8)
+        arrived(sq.at[from_z % 4], sq_r.at[j - 1], from_z // 4 == l)
     qpart = jnp.zeros((QR, GC), F32)
     for m in range(2):
         zero = jnp.zeros((QR, 384), F32)
         first = jnp.concatenate([sq[2 * m].astype(F32), zero], axis=1)
         second = jnp.concatenate([sq[2 * m + 1].astype(F32), zero], axis=1)
         both = (first + pltpu.roll(second, GC, 1))[:, 0:640].astype(BF)
-        qpart += lax.dot_general(both, ebuf[m], (((1,), (1,)), ((), ())), preferred_element_type=F32)
+        qpart += lax.dot_general(both, ebuf[(x * 4 + l * 2) + m], (((1,), (1,)), ((), ())),
+                                 preferred_element_type=F32)
     qpb[chip] = jnp.concatenate([qpart, jnp.zeros((QR, 64), F32)], axis=1)
     for b in range(8):
         send(qpb.at[chip], qpb.at[chip], rq_s.at[b], rq_r.at[chip], device(b % 4, b // 4, k, h, z), chip != b)
+
+    s_got(0, 4)
+    s_got(1, 4)
+    rgb[...] = (acc[...] + s_dot(order[3])).astype(BF)
+
+    def rg_slot(s):
+        return rg.at[:, pl.ds(pl.multiple_of(s * 128, 128), 128)]
+
+    for b in range(8):
+        send(rgb, rg_slot(shard), ag_s.at[b], ag_r.at[chip], device(b % 4, b // 4, k, h, z), chip != b)
+    send(rgb, rg_slot(shard), fw_s.at[chip], fw_r.at[chip], core)
+    own_rg = local(rgb, rg_slot(shard), loc.at[4])
 
     r_got(1)
     r_ring(2)
@@ -351,23 +382,6 @@
     send(raq_slot(pos), raq_slot(pos), rk_s.at[2], rk_r.at[2], up, held(pos))
     pos = mod(z + 1, 8)
     arrived(raq_slot(pos), rk_r.at[1], held(pos))
-
-    rsb[chip] = pb[chip]
-    for b in range(8):
-        arrived(rsb.at[b], rs_r.at[b], chip != b)
-    block = rsb[0].astype(F32)
-    for b in range(1, 8):
-        block += rsb[b].astype(F32)
-    rgb[...] = block.astype(BF)
-
-    def rg_slot(s):
-        return rg.at[:, pl.ds(pl.multiple_of(s * 128, 128), 128)]
-
-    for b in range(8):
-        send(rgb, rg_slot(shard), ag_s.at[b], ag_r.at[chip], device(b % 4, b // 4, k, h, z), chip != b)
-    send(rgb, rg_slot(shard), fw_s.at[chip], fw_r.at[chip], core)
-    own_rg = pltpu.make_async_copy(rgb, rg_slot(shard), loc.at[4])
-    own_rg.start()
 
     r_got(2)
     r_ring(3)
@@ -462,20 +476,20 @@
 
 def per_device(train_act, train_grad, query_act, query_grad, query_of, counts, eig_act, eig_grad):
     vm = pl.BlockSpec(memory_space=pltpu.VMEM)
-    sm = pl.BlockSpec(memory_space=pltpu.SMEM)
+    hb = pl.BlockSpec(memory_space=pltpu.HBM)
     V = pltpu.VMEM
     dma = pltpu.SemaphoreType.DMA
     scratch = [
-        V((AR, AC), BF), V((AR, D), BF), V((D, AC), BF), V((2, GC, 640), BF),
-        V((4, GC, TOK), BF), V((QR, 384), BF), V((QR, 384), BF), V((2, 1280, 512), BF), V((4, QR, 384), BF),
-        V((2, GC, 512), F32), V((8, GC, TOK), BF), V((8, GC, TOK), BF), V((8, QR, 384), F32),
-        V((GC, TOK), BF), V((GC, 2048), BF),
+        pltpu.SMEM((QR,), jnp.int32), pltpu.SMEM((16,), jnp.int32), V((QR, GC), BF), V((GC, TOK), BF), dma((11,)),
+        V((AR, AC), BF), V((AR, D), BF), V((8, 4, AC, AC), BF), V((16, GC, 640), BF),
+        V((QR, 384), BF), V((4, 8 * GC, TOK), BF), V((4, QR, 384), BF),
+        V((GC, TOK), F32), V((8, QR, 384), F32), V((GC, TOK), BF), V((GC, 2048), BF),
         V((AR, AC), BF), V((4, AR, AC), BF), V((2, 1024, 256), BF), V((QR, 256), BF),
         V((QUERIES, GC, 256), BF), V((8, 2048), F32), V((16, 8, 128), F32), V((4, 8, 128), F32), V((8, 8, 128), F32),
     ]
     counts_of = [
-        (4,), (4,), (2, 4), (2, 4), (), (), (2,), (2,), (7,), (4,), (4,), (4,),
-        (2, 2, 4), (2, 2, 4), (3,), (3,), (8,), (8,), (8,), (8,), (8,), (8,), (8,), (8,),
+        (4,), (4,), (2, 4), (2, 4), (8,), (8,), (9,), (9,), (4,), (4,),
+        (2, 2, 4), (2, 2, 4), (11,), (8,), (8,), (8,), (8,), (8,), (8,), (8,),
         (), (), (4,), (4,), (8,), (8,), (2, 2, 4), (2, 2, 4), (3,), (3,),
         (16,), (16,), (4,), (4,), (8,), (8,), (5,),
     ]
@@ -483,12 +497,12 @@
     scores, corr = pl.pallas_call(
         kernel,
         out_shape=(jax.ShapeDtypeStruct((8, 128), F32), jax.ShapeDtypeStruct((GC, 256), F32)),
-        in_specs=[vm, vm, vm, vm, sm, sm, vm, vm],
+        in_specs=[hb] * 8,
         out_specs=(vm, vm),
         scratch_shapes=scratch,
         compiler_params=pltpu.CompilerParams(
             collective_id=0, has_side_effects=True, vmem_limit_bytes=48 * 2**20),
-    )(train_act, train_grad.T, query_act, query_grad, query_of, counts, eig_act, eig_grad.T)
+    )(train_act, train_grad.T, query_act, query_grad, query_of, counts, eig_act.reshape(4, 8, AC, AC), eig_grad.T)
     return scores[:, :4], corr.T
 
 

time: 123 us -> 123 us (level)
  the two profiles are of different devices: /device:TPU:16 before, /device:TPU:8 now
where the time goes in v2:
time: 123 us
  Pallas kernels  116 us (94%)
  local copies, waits for them, and re-layouts  6.62 us (5%)
    pallas_call x1, Pallas kernels, per_device(): pl.pallas_call(kernel, out_shape=(jax.ShapeDtypeStruct((8, 128), F32), ja...  116 us
    unnamed x18, local copies, waits for them, and re-layouts  6.62 us

profile of v2, /device:TPU:8, one launch (start us, length us, event | category | flops | bytes accessed | tf_op | source)
XLA Modules:
  0.0 122.9 jit_solution(17630583918046937012)
XLA Ops:
  0.6 0.0 copy-start.5
  0.6 0.0 copy-start.6
  0.7 0.0 copy-start.7
  0.7 0.7 copy-done.5
  1.3 0.0 copy-done.6
  1.3 0.0 copy-done.7
  1.3 0.0 copy-start
  1.3 1.2 copy-done
  2.6 0.0 copy-start.1
  2.6 1.0 copy-done.1
  3.6 0.0 copy-start.2
  3.6 0.9 copy-done.2
  4.4 0.0 copy-start.3
  4.4 0.8 copy-done.3
  5.2 0.0 copy-start.4
  5.2 0.7 copy-done.4
  5.9 115.6 %shard_map.95 = (f32[8,128]{1,0:T(8,128)S(1)}, f32[320,256]{1,0:T(8,128)S(1)}) custom-call(bf16[128,128]{1,0:T(8,128)(2,1)S(1)} %copy-done.3, bf16[320,128]{1,0:T(8,128)(2,1)S(1)} %bitcast.8, bf16[16,128]{1,0:T(8,128)(2,1)S(1)} %copy-done.5, bf16[16,320]{1,0:T(8,128)(2,1)S(1)} %copy-done.4, s32[16]{0:T(128)S(1)} %copy-done.6, s32[16]{0:T(128)S(1)} %copy-done.7, ...), custom_call_target="tpu_custom_call" | custom-call | tf_op jit(solution)/shard_map/pallas_call | solution.py:497
  121.5 0.7 copy.10
  122.1 0.7 copy.12
Async XLA Ops:
  0.6 0.7 copy-start.5
  0.6 0.7 copy-start.6
  0.7 0.7 copy-start.7
  1.3 1.2 copy-start
  2.6 1.0 copy-start.1
  3.6 0.9 copy-start.2
  4.4 0.8 copy-start.3
  5.2 0.7 copy-start.4

commit v3 on v2

--- a/solution.py
+++ b/solution.py
@@ -23,6 +23,8 @@
 GC = 320
 QR = 16
 AR = TOK + QR
+AY = 80
+GY = 240
 
 
 def mod(value, size):
@@ -34,9 +36,10 @@
 
 
 def kernel(ta, tg, qa, qg, qof_in, cnt_in, ea, eg, sc_out, corr_out,
-           qof, cnt, qgv, tgv, ld, blk_a, act, ea2, ebuf, qmsg, gbuf, sq, acc, qpb, rgb, rg,
+           qof, cnt, qgv, ld, act, ea2, ebuf, qmsg, gbuf, sq, acc, qpb, rgb, rg,
            rab, rs1, ra, raq, wts, fsc, f1, f2, f3, *sems):
     (a_s, a_r, ar_s, ar_r, ec_s, ec_r, ex_s, ex_r, s1_s, s1_r,
+     az_s, az_r, gz_s, gz_r, c_s, c_r, gc_s, gc_r,
      sr_s, sr_r, sq_s, sq_r, rq_s, rq_r, ag_s, ag_r, fw_s, fw_r,
      r0_s, r0_r, r1_s, r1_r, r2_s, r2_r, rr_s, rr_r, rk_s, rk_r,
      f1_s, f1_r, f2_s, f2_r, f3_s, f3_r, loc) = sems
@@ -93,8 +96,9 @@
         c.start()
         return c
 
-    loads = [local(ta, blk_a.at[pl.ds(0, TOK), :], ld.at[0]), local(qa, blk_a.at[pl.ds(TOK, QR), :], ld.at[1]),
-             local(qg, qgv, ld.at[2]), local(tg, tgv, ld.at[3]), local(eg, ebuf.at[dp], ld.at[4]),
+    loads = [local(ta, act.at[h, z, pl.ds(0, TOK), :], ld.at[0]),
+             local(qa, act.at[h, z, pl.ds(TOK, QR), :], ld.at[1]),
+             local(qg, qgv, ld.at[2]), local(tg, gbuf.at[h, z], ld.at[3]), local(eg, ebuf.at[dp], ld.at[4]),
              local(qof_in, qof, ld.at[5]), local(cnt_in, cnt, ld.at[6])]
     loads += [local(ea.at[hh], ea2.at[:, hh], ld.at[7 + hh]) for hh in range(4)]
     for c in loads:
@@ -110,25 +114,51 @@
     def _():
         pl.semaphore_wait(bar, len(peers))
 
-    def act_slot(pos, lo=0, n=4):
-        return act.at[:, pl.ds(pl.multiple_of(pos * 512 + lo * 128, 128), n * 128)]
-
-    def act_one(pos, hh):
-        return act.at[:, pl.ds(pl.multiple_of(pos * 512 + hh * 128, 128), 128)]
-
-    for j in range(1, 4):
-        send(blk_a, act_one(z, h), a_s.at[j], a_r.at[j], device(x, l, k, mod(h + j, 4), z))
-    own_act = local(blk_a, act_one(z, h), loc.at[0])
-
-    def g_one(pos, hh):
-        return gbuf.at[hh, pl.ds(pl.multiple_of(pos * GC, GC), GC), :]
-
-    def g_slot(pos, half):
-        return gbuf.at[pl.ds(half * 2, 2), pl.ds(pl.multiple_of(pos * GC, GC), GC), :]
-
-    for j in range(1, 4):
-        send(tgv, g_one(z, h), s1_s.at[j], s1_r.at[j], device(x, l, k, mod(h + j, 4), z))
-    own_g = local(tgv, g_one(z, h), loc.at[1])
+    hp, hm, ho = mod(h + 1, 4), mod(h - 1, 4), mod(h + 2, 4)
+    above, below = device(x, l, k, hp, z), device(x, l, k, hm, z)
+
+    def y_out(get, ss, rs):
+        send(get(h, None), get(h, None), ss.at[0], rs.at[0], above)
+        send(get(h, None), get(h, None), ss.at[1], rs.at[1], below)
+
+    def y_mid(get, ss, rs):
+        arrived(get(hm, None), rs.at[0])
+        send(get(hm, 0), get(hm, 0), ss.at[2], rs.at[2], above)
+        arrived(get(hp, None), rs.at[1])
+        send(get(hp, 1), get(hp, 1), ss.at[3], rs.at[3], below)
+
+    def y_in(get, rs):
+        arrived(get(ho, 0), rs.at[2])
+        arrived(get(ho, 1), rs.at[3])
+
+    def act_y(hh, part):
+        lo, n = ((0, AY), (0, 48), (48, AY - 48))[0 if part is None else part + 1]
+        return act.at[hh, z, pl.ds(lo, n), :]
+
+    def g_y(hh, part):
+        lo, n = ((0, GY), (0, 128), (128, GY - 128))[0 if part is None else part + 1]
+        return gbuf.at[hh, z, pl.ds(lo, n), :]
+
+    def act_col(hh, part):
+        zs = pl.ds(0, 8) if part is None else pl.ds(4 * part, 4)
+        return act.at[hh, zs, pl.ds(AY, AR - AY), :]
+
+    def g_col(hh, part):
+        zs = pl.ds(0, 8) if part is None else pl.ds(4 * part, 4)
+        return gbuf.at[hh, zs, pl.ds(GY, GC - GY), :]
+
+    def act_z(pos):
+        return act.at[h, pos, pl.ds(AY, AR - AY), :]
+
+    def g_z(pos):
+        return gbuf.at[h, pos, pl.ds(GY, GC - GY), :]
+
+    y_out(act_y, a_s, a_r)
+    y_out(g_y, s1_s, s1_r)
+    for j in (1, 7, 2, 6, 3, 5, 4):
+        send(act_z(z), act_z(z), az_s.at[j], az_r.at[j], device(x, l, k, h, mod(z + j, 8)))
+    for j in (1, 7, 2, 6, 3, 5, 4):
+        send(g_z(z), g_z(z), gz_s.at[j], gz_r.at[j], device(x, l, k, h, mod(z + j, 8)))
 
     for j in range(1, 4):
         send(qmsg, sq.at[zr], sq_s.at[j], sq_r.at[7], device(x, l, k, mod(h + j, 4), z),
@@ -156,9 +186,11 @@
     send(e_at(x, l), e_at(x, l), ex_s.at[2], ex_r.at[2], left)
     e_pass(x, l, 0)
 
-    own_act.wait()
-    for j in range(1, 4):
-        arrived(act_one(z, mod(h - j, 4)), a_r.at[j])
+    def act_slot(pos, lo=0, n=4):
+        return act.at[pl.ds(lo, n), pos, pl.ds(0, AY), :]
+
+    def g_slot(pos, half):
+        return gbuf.at[pl.ds(half * 2, 2), pos, pl.ds(0, GY), :]
 
     def act_ring(hop):
         n = 4 if hop < 4 else 2
@@ -174,9 +206,13 @@
         arrived(act_slot(mod(z + hop, 8), 4 - n, n), ar_r.at[1, hop - 1])
 
     def act_dot(pos):
-        return jnp.dot(act[:, pl.ds(pl.multiple_of(pos * 512, 512), 512)],
-                       ea2[pos].reshape(512, 128),
-                       preferred_element_type=F32)
+        lhs = jnp.concatenate([act[hh, pos, 0:AY, :] for hh in range(4)], axis=1)
+        return jnp.dot(lhs, ea2[pos].reshape(512, AC), preferred_element_type=F32)
+
+    def act_dot2(hh):
+        lhs = jnp.concatenate([act[hh, zz, AY:AR, :] for zz in range(8)], axis=1)
+        rhs = jnp.concatenate([ea2[zz, hh] for zz in range(8)], axis=0)
+        return jnp.dot(lhs, rhs, preferred_element_type=F32)
 
     def s_ring(half, hop):
         if hop < 4 or half == 0:
@@ -192,19 +228,27 @@
         if hop < 4 or half == 1:
             arrived(g_slot(mod(z + hop, 8), half), sr_r.at[1, half, hop - 1])
 
+    y_mid(act_y, a_s, a_r)
+    y_mid(g_y, s1_s, s1_r)
+    y_in(act_y, a_r)
     act_ring(1)
+    for j in range(1, 8):
+        arrived(act_z(mod(z - j, 8)), az_r.at[j])
+    y_out(act_col, c_s, c_r)
     total = act_dot(z)
-    own_g.wait()
-    for j in range(1, 4):
-        arrived(g_one(z, mod(h - j, 4)), s1_r.at[j])
+    y_in(g_y, s1_r)
     s_ring(0, 1)
     s_ring(1, 1)
+    act_got(1)
+    act_ring(2)
     arrived(sq.at[zr], sq_r.at[7], jnp.logical_and(h != x, za == l))
     for j in range(1, 8):
         send(sq.at[zr], sq.at[zr], sq_s.at[3 + j], sq_r.at[j - 1],
              device(x, l, k, h, mod(z + j, 8)), za == l)
-    act_got(1)
-    act_ring(2)
+    for j in range(1, 8):
+        arrived(g_z(mod(z - j, 8)), gz_r.at[j])
+    y_mid(act_col, c_s, c_r)
+    y_out(g_col, gc_s, gc_r)
     total += act_dot(mod(z - 1, 8)) + act_dot(mod(z + 1, 8))
 
     arrived(e_at(x, 1 - l), ex_r.at[0])
@@ -225,13 +269,17 @@
     act_got(3)
     act_ring(4)
     total += act_dot(mod(z - 3, 8)) + act_dot(mod(z + 3, 8))
+    total2 = act_dot2(h) + act_dot2(hm) + act_dot2(hp)
     s_got(0, 1)
     s_ring(0, 2)
     s_got(1, 1)
     s_ring(1, 2)
+    y_in(act_col, c_r)
+    total2 += act_dot2(ho)
     act_got(4)
     total += act_dot(mod(z + 4, 8))
-    rab[...] = total.astype(BF)
+    rab[0:AY, :] = total.astype(BF)
+    rab[AY:AR, :] = total2.astype(BF)
 
     send(rab, rs1.at[h], r0_s, r0_r, partner, swap)
 
@@ -239,6 +287,7 @@
     def _():
         rs1[h] = rab[...]
 
+    y_mid(g_col, gc_s, gc_r)
     arrived(e_at(xm, 1 - l), ex_r.at[3])
     send(e_at(xm, 1 - l, 0), e_at(xm, 1 - l, 0), ex_s.at[7], ex_r.at[7], right)
     e_pass(xm, 1 - l, 4)
@@ -246,17 +295,21 @@
     send(e_at(xp, 1 - l, 1), e_at(xp, 1 - l, 1), ex_s.at[8], ex_r.at[8], left)
     e_pass(xp, 1 - l, 5)
 
+    def rs_at(hh, part):
+        lo, n = ((0, AR), (0, 80), (80, 64))[0 if part is None else part + 1]
+        return rs1.at[hh, pl.ds(lo, n), :]
+
     arrived(rs1.at[h], r0_r, swap)
-    for j in range(1, 4):
-        send(rs1.at[h], rs1.at[h], r1_s.at[j], r1_r.at[j], device(x, l, k, mod(h + j, 4), z))
+    y_out(rs_at, r1_s, r1_r)
 
     s_got(0, 2)
     s_ring(0, 3)
     s_got(1, 2)
     s_ring(1, 3)
-
-    for j in range(1, 4):
-        arrived(rs1.at[mod(h - j, 4)], r1_r.at[j])
+    y_mid(rs_at, r1_s, r1_r)
+    y_in(g_col, gc_r)
+    y_in(rs_at, r1_r)
+
     kt = zr // 2
     mine = k == kt
 
@@ -341,7 +394,7 @@
     def s_dot(n):
         out = jnp.zeros((GC, TOK), F32)
         for hh in range(4):
-            out += jnp.dot(ebuf[hh * 4 + n], gbuf[hh, pl.ds(pl.multiple_of(n * 640, 640), 640), :],
+            out += jnp.dot(ebuf[hh * 4 + n], gbuf[hh, pl.ds(2 * n, 2)].reshape(640, TOK),
                            preferred_element_type=F32)
         return out
 
@@ -429,21 +482,18 @@
         prod = jnp.dot(picked, raq[...], preferred_element_type=F32)
         wts[q] = (prod / corr_out[...]).astype(BF)
 
-    def chunk(c, carry):
-        rac = ra[c // 4, pl.ds(pl.multiple_of((c % 4) * 256, 256), 256), :]
-        rgc = rg[:, pl.ds(pl.multiple_of(c * 256, 256), 256)].astype(F32)
+    for c in range(8):
+        rac = ra[c // 4, (c % 4) * 256:(c % 4) * 256 + 256, :]
+        rgc = rg[:, c * 256:c * 256 + 256].astype(F32)
         rows = []
         for q in range(QUERIES):
             mixed = lax.dot_general(wts[q], rac, (((1,), (1,)), ((), ())), preferred_element_type=F32)
             rows.append(jnp.sum(mixed * rgc, axis=0, keepdims=True))
-        fsc[:, pl.ds(pl.multiple_of(c * 256, 256), 256)] = jnp.concatenate(rows, axis=0)
-        return carry
-
-    lax.fori_loop(0, 8, chunk, 0)
-
-    for s in range(16):
-        send(fsc.at[:, pl.ds(s * 128, 128)], f1.at[shard], f1_s.at[s], f1_r.at[shard],
-             device((s // 2) % 4, s // 8, s % 2, h, z), shard != s)
+        fsc[:, c * 256:c * 256 + 256] = jnp.concatenate(rows, axis=0)
+        for s in (2 * c, 2 * c + 1):
+            send(fsc.at[:, pl.ds(s * 128, 128)], f1.at[shard], f1_s.at[s], f1_r.at[shard],
+                 device((s // 2) % 4, s // 8, s % 2, h, z), shard != s)
+
     f1[shard] = fsc[:, pl.ds(pl.multiple_of(shard * 128, 128), 128)]
     for s in range(16):
         arrived(f1.at[s], f1_r.at[s], shard != s)
@@ -480,15 +530,16 @@
     V = pltpu.VMEM
     dma = pltpu.SemaphoreType.DMA
     scratch = [
-        pltpu.SMEM((QR,), jnp.int32), pltpu.SMEM((16,), jnp.int32), V((QR, GC), BF), V((GC, TOK), BF), dma((11,)),
-        V((AR, AC), BF), V((AR, D), BF), V((8, 4, AC, AC), BF), V((16, GC, 640), BF),
-        V((QR, 384), BF), V((4, 8 * GC, TOK), BF), V((4, QR, 384), BF),
+        pltpu.SMEM((QR,), jnp.int32), pltpu.SMEM((16,), jnp.int32), V((QR, GC), BF), dma((11,)),
+        V((4, 8, AR, AC), BF), V((8, 4, AC, AC), BF), V((16, GC, 640), BF),
+        V((QR, 384), BF), V((4, 8, GC, TOK), BF), V((4, QR, 384), BF),
         V((GC, TOK), F32), V((8, QR, 384), F32), V((GC, TOK), BF), V((GC, 2048), BF),
         V((AR, AC), BF), V((4, AR, AC), BF), V((2, 1024, 256), BF), V((QR, 256), BF),
         V((QUERIES, GC, 256), BF), V((8, 2048), F32), V((16, 8, 128), F32), V((4, 8, 128), F32), V((8, 8, 128), F32),
     ]
     counts_of = [
         (4,), (4,), (2, 4), (2, 4), (8,), (8,), (9,), (9,), (4,), (4,),
+        (8,), (8,), (8,), (8,), (4,), (4,), (4,), (4,),
         (2, 2, 4), (2, 2, 4), (11,), (8,), (8,), (8,), (8,), (8,), (8,), (8,),
         (), (), (4,), (4,), (8,), (8,), (2, 2, 4), (2, 2, 4), (3,), (3,),
         (16,), (16,), (4,), (4,), (8,), (8,), (5,),

time: 123 us -> 124 us (level)
  the two profiles are of different devices: /device:TPU:8 before, /device:TPU:14 now
where the time goes in v3:
time: 124 us
  Pallas kernels  117 us (94%)
  local copies, waits for them, and re-layouts  6.62 us (5%)
    pallas_call x1, Pallas kernels, per_device(): pl.pallas_call(kernel, out_shape=(jax.ShapeDtypeStruct((8, 128), F32), ja...  117 us
    unnamed x18, local copies, waits for them, and re-layouts  6.62 us

profile of v3, /device:TPU:14, one launch (start us, length us, event | category | flops | bytes accessed | tf_op | source)
XLA Modules:
  0.0 124.0 jit_solution(1211639487287828032)
XLA Ops:
  0.6 0.0 copy-start.5
  0.6 0.0 copy-start.6
  0.7 0.0 copy-start.7
  0.7 0.7 copy-done.5
  1.3 0.0 copy-done.6
  1.3 0.0 copy-done.7
  1.3 0.0 copy-start
  1.3 1.2 copy-done
  2.6 0.0 copy-start.1
  2.6 1.0 copy-done.1
  3.6 0.0 copy-start.2
  3.6 0.9 copy-done.2
  4.4 0.0 copy-start.3
  4.4 0.8 copy-done.3
  5.2 0.0 copy-start.4
  5.2 0.7 copy-done.4
  5.9 116.7 %shard_map.95 = (f32[8,128]{1,0:T(8,128)S(1)}, f32[320,256]{1,0:T(8,128)S(1)}) custom-call(bf16[128,128]{1,0:T(8,128)(2,1)S(1)} %copy-done.3, bf16[320,128]{1,0:T(8,128)(2,1)S(1)} %bitcast.8, bf16[16,128]{1,0:T(8,128)(2,1)S(1)} %copy-done.5, bf16[16,320]{1,0:T(8,128)(2,1)S(1)} %copy-done.4, s32[16]{0:T(128)S(1)} %copy-done.6, s32[16]{0:T(128)S(1)} %copy-done.7, ...), custom_call_target="tpu_custom_call" | custom-call | tf_op jit(solution)/shard_map/pallas_call | solution.py:548
  122.6 0.7 copy.10
  123.3 0.7 copy.12
Async XLA Ops:
  0.6 0.7 copy-start.5
  0.6 0.7 copy-start.6
  0.7 0.7 copy-start.7
  1.3 1.2 copy-start
  2.6 1.0 copy-start.1
  3.6 0.9 copy-start.2
  4.4 0.8 copy-start.3
  5.2 0.7 copy-start.4

commit v4 on v3

--- a/solution.py
+++ b/solution.py
@@ -76,6 +76,14 @@
         else:
             pl.when(when)(lambda: c.wait_recv())
 
+    def flush():
+        for c, when in pending:
+            if when is None:
+                c.wait_send()
+            else:
+                pl.when(when)(functools.partial(lambda c: c.wait_send(), c))
+        pending.clear()
+
     bar = pltpu.get_barrier_semaphore()
     peers = [device(x, l, k, mod(h + j, 4), z) for j in range(1, 4)]
     peers += [device(x, l, k, h, mod(z + j, 8)) for j in range(1, 8)]
@@ -229,53 +237,51 @@
             arrived(g_slot(mod(z + hop, 8), half), sr_r.at[1, half, hop - 1])
 
     y_mid(act_y, a_s, a_r)
+    for j in range(1, 8):
+        arrived(act_z(mod(z - j, 8)), az_r.at[j])
+    y_out(act_col, c_s, c_r)
     y_mid(g_y, s1_s, s1_r)
     y_in(act_y, a_r)
     act_ring(1)
-    for j in range(1, 8):
-        arrived(act_z(mod(z - j, 8)), az_r.at[j])
-    y_out(act_col, c_s, c_r)
-    total = act_dot(z)
     y_in(g_y, s1_r)
     s_ring(0, 1)
     s_ring(1, 1)
+    for j in range(1, 8):
+        arrived(g_z(mod(z - j, 8)), gz_r.at[j])
+    y_out(g_col, gc_s, gc_r)
+    arrived(sq.at[zr], sq_r.at[7], jnp.logical_and(h != x, za == l))
+    for j in range(1, 8):
+        send(sq.at[zr], sq.at[zr], sq_s.at[3 + j], sq_r.at[j - 1],
+             device(x, l, k, h, mod(z + j, 8)), za == l)
+    total = act_dot(z)
     act_got(1)
     act_ring(2)
-    arrived(sq.at[zr], sq_r.at[7], jnp.logical_and(h != x, za == l))
-    for j in range(1, 8):
-        send(sq.at[zr], sq.at[zr], sq_s.at[3 + j], sq_r.at[j - 1],
-             device(x, l, k, h, mod(z + j, 8)), za == l)
-    for j in range(1, 8):
-        arrived(g_z(mod(z - j, 8)), gz_r.at[j])
-    y_mid(act_col, c_s, c_r)
-    y_out(g_col, gc_s, gc_r)
     total += act_dot(mod(z - 1, 8)) + act_dot(mod(z + 1, 8))
 
     arrived(e_at(x, 1 - l), ex_r.at[0])
     send(e_at(x, 1 - l), e_at(x, 1 - l), ex_s.at[3], ex_r.at[3], right)
     send(e_at(x, 1 - l), e_at(x, 1 - l), ex_s.at[4], ex_r.at[4], left)
     e_pass(x, 1 - l, 1)
-    act_got(2)
-    act_ring(3)
-    total += act_dot(mod(z - 2, 8)) + act_dot(mod(z + 2, 8))
-
     arrived(e_at(xm, l), ex_r.at[1])
     send(e_at(xm, l, 0), e_at(xm, l, 0), ex_s.at[5], ex_r.at[5], right)
     e_pass(xm, l, 2)
     arrived(e_at(xp, l), ex_r.at[2])
     send(e_at(xp, l, 1), e_at(xp, l, 1), ex_s.at[6], ex_r.at[6], left)
     e_pass(xp, l, 3)
-
-    act_got(3)
-    act_ring(4)
-    total += act_dot(mod(z - 3, 8)) + act_dot(mod(z + 3, 8))
-    total2 = act_dot2(h) + act_dot2(hm) + act_dot2(hp)
+    y_mid(act_col, c_s, c_r)
+    act_got(2)
+    act_ring(3)
+    total2 = act_dot2(h)
     s_got(0, 1)
     s_ring(0, 2)
     s_got(1, 1)
     s_ring(1, 2)
+    total += act_dot(mod(z - 2, 8)) + act_dot(mod(z + 2, 8))
+    act_got(3)
+    act_ring(4)
     y_in(act_col, c_r)
-    total2 += act_dot2(ho)
+    total += act_dot(mod(z - 3, 8)) + act_dot(mod(z + 3, 8))
+    total2 += act_dot2(hm) + act_dot2(hp) + act_dot2(ho)
     act_got(4)
     total += act_dot(mod(z + 4, 8))
     rab[0:AY, :] = total.astype(BF)
@@ -288,6 +294,14 @@
         rs1[h] = rab[...]
 
     y_mid(g_col, gc_s, gc_r)
+    s_got(0, 2)
+    s_ring(0, 3)
+    s_got(1, 2)
+    s_ring(1, 3)
+
+    arrived(rs1.at[h], r0_r, swap)
+    for j in range(1, 4):
+        send(rs1.at[h], rs1.at[h], r1_s.at[j], r1_r.at[j], device(x, l, k, mod(h + j, 4), z))
     arrived(e_at(xm, 1 - l), ex_r.at[3])
     send(e_at(xm, 1 - l, 0), e_at(xm, 1 - l, 0), ex_s.at[7], ex_r.at[7], right)
     e_pass(xm, 1 - l, 4)
@@ -295,21 +309,8 @@
     send(e_at(xp, 1 - l, 1), e_at(xp, 1 - l, 1), ex_s.at[8], ex_r.at[8], left)
     e_pass(xp, 1 - l, 5)
 
-    def rs_at(hh, part):
-        lo, n = ((0, AR), (0, 80), (80, 64))[0 if part is None else part + 1]
-        return rs1.at[hh, pl.ds(lo, n), :]
-
-    arrived(rs1.at[h], r0_r, swap)
-    y_out(rs_at, r1_s, r1_r)
-
-    s_got(0, 2)
-    s_ring(0, 3)
-    s_got(1, 2)
-    s_ring(1, 3)
-    y_mid(rs_at, r1_s, r1_r)
-    y_in(g_col, gc_r)
-    y_in(rs_at, r1_r)
-
+    for j in range(1, 4):
+        arrived(rs1.at[mod(h - j, 4)], r1_r.at[j])
     kt = zr // 2
     mine = k == kt
 
@@ -340,18 +341,13 @@
         a.wait()
         b.wait()
 
-    arrived(e_at(xo, l, 0), ex_r.at[5])
-    arrived(e_at(xo, l, 1), ex_r.at[6])
-    e_pass(xo, l, 6)
-    arrived(e_at(xo, 1 - l, 0), ex_r.at[7])
-    arrived(e_at(xo, 1 - l, 1), ex_r.at[8])
-    e_pass(xo, 1 - l, 7)
-
     s_got(0, 3)
     s_ring(0, 4)
     s_got(1, 3)
     s_ring(1, 4)
-
+    arrived(e_at(xo, l, 0), ex_r.at[5])
+    arrived(e_at(xo, l, 1), ex_r.at[6])
+    e_pass(xo, l, 6)
     for j in range(1, 4):
         arrived(ra_block(z, mod(x - j, 4), k), r2_r.at[j], mine)
     for j in range(4):
@@ -384,6 +380,11 @@
     send(raq_slot(z), raq_slot(z), rk_s.at[0], rk_r.at[0], up, held(z))
     send(raq_slot(z), raq_slot(z), rk_s.at[1], rk_r.at[1], down, held(z))
 
+    arrived(e_at(xo, 1 - l, 0), ex_r.at[7])
+    arrived(e_at(xo, 1 - l, 1), ex_r.at[8])
+    e_pass(xo, 1 - l, 7)
+    y_in(g_col, gc_r)
+
     e_of = [(x, l), (x, 1 - l), (xm, l), (xp, l), (xm, 1 - l), (xp, 1 - l), (xo, l), (xo, 1 - l)]
     for i, (xx, ll) in enumerate(e_of):
         arrived(ebuf.at[xx * 4 + ll * 2 + 1 - k], ec_r.at[i])
@@ -400,6 +401,25 @@
 
     acc[...] = s_dot(order[0]) + s_dot(order[1])
     acc[...] += s_dot(order[2])
+    s_got(0, 4)
+    s_got(1, 4)
+    rgb[...] = (acc[...] + s_dot(order[3])).astype(BF)
+
+    def rg_slot(s):
+        return rg.at[:, pl.ds(pl.multiple_of(s * 128, 128), 128)]
+
+    for b in range(8):
+        send(rgb, rg_slot(shard), ag_s.at[b], ag_r.at[chip], device(b % 4, b // 4, k, h, z), chip != b)
+    send(rgb, rg_slot(shard), fw_s.at[chip], fw_r.at[chip], core)
+    own_rg = local(rgb, rg_slot(shard), loc.at[4])
+
+    r_got(1)
+    r_ring(2)
+    pos = mod(z - 1, 8)
+    arrived(raq_slot(pos), rk_r.at[0], held(pos))
+    send(raq_slot(pos), raq_slot(pos), rk_s.at[2], rk_r.at[2], up, held(pos))
+    pos = mod(z + 1, 8)
+    arrived(raq_slot(pos), rk_r.at[1], held(pos))
 
     for j in range(1, 8):
         from_z = mod(z - j, 8)
@@ -415,26 +435,6 @@
     qpb[chip] = jnp.concatenate([qpart, jnp.zeros((QR, 64), F32)], axis=1)
     for b in range(8):
         send(qpb.at[chip], qpb.at[chip], rq_s.at[b], rq_r.at[chip], device(b % 4, b // 4, k, h, z), chip != b)
-
-    s_got(0, 4)
-    s_got(1, 4)
-    rgb[...] = (acc[...] + s_dot(order[3])).astype(BF)
-
-    def rg_slot(s):
-        return rg.at[:, pl.ds(pl.multiple_of(s * 128, 128), 128)]
-
-    for b in range(8):
-        send(rgb, rg_slot(shard), ag_s.at[b], ag_r.at[chip], device(b % 4, b // 4, k, h, z), chip != b)
-    send(rgb, rg_slot(shard), fw_s.at[chip], fw_r.at[chip], core)
-    own_rg = local(rgb, rg_slot(shard), loc.at[4])
-
-    r_got(1)
-    r_ring(2)
-    pos = mod(z - 1, 8)
-    arrived(raq_slot(pos), rk_r.at[0], held(pos))
-    send(raq_slot(pos), raq_slot(pos), rk_s.at[2], rk_r.at[2], up, held(pos))
-    pos = mod(z + 1, 8)
-    arrived(raq_slot(pos), rk_r.at[1], held(pos))
 
     r_got(2)
     r_ring(3)
@@ -517,11 +517,7 @@
     done = jnp.where(t < cnt[dp], done, 0.0) * (1.0 / math.sqrt(D * FF * QTOK))
     sc_out[...] = pltpu.roll(done, mod(128 - 4 * owner, 128), 1)
 
-    for c, when in pending:
-        if when is None:
-            c.wait_send()
-        else:
-            pl.when(when)(functools.partial(lambda c: c.wait_send(), c))
+    flush()
 
 
 def per_device(train_act, train_grad, query_act, query_grad, query_of, counts, eig_act, eig_grad):
@@ -552,7 +548,7 @@
         out_specs=(vm, vm),
         scratch_shapes=scratch,
         compiler_params=pltpu.CompilerParams(
-            collective_id=0, has_side_effects=True, vmem_limit_bytes=48 * 2**20),
+            collective_id=0, has_side_effects=True, vmem_limit_bytes=60 * 2**20),
     )(train_act, train_grad.T, query_act, query_grad, query_of, counts, eig_act.reshape(4, 8, AC, AC), eig_grad.T)
     return scores[:, :4], corr.T
 

time: 124 us -> 122 us (0.984)
  local copies, waits for them, and re-layouts: 6.62 us -> 3.03 us
    unnamed x18 -> x4, local copies, waits for them, and re-layouts: 6.62 us -> 3.03 us
    pallas_call x1, Pallas kernels: 117 us -> 118 us  [per_device(): pl.pallas_call(kernel, out_shape=(jax.ShapeDtypeStruct((8, 128), F32), ja...]
where the time goes in v4:
time: 122 us
  Pallas kernels  118 us (97%)
  local copies, waits for them, and re-layouts  3.03 us (2%)
    pallas_call x1, Pallas kernels, per_device(): pl.pallas_call(kernel, out_shape=(jax.ShapeDtypeStruct((8, 128), F32), ja...  118 us
    unnamed x4, local copies, waits for them, and re-layouts  3.03 us

profile of v4, /device:TPU:14, one launch (start us, length us, event | category | flops | bytes accessed | tf_op | source)
XLA Modules:
  0.0 121.8 jit_solution(2577604943952495038)
XLA Ops:
  0.6 118.1 %shard_map.95 = (f32[8,128]{1,0:T(8,128)}, f32[320,256]{1,0:T(8,128)}) custom-call(bf16[128,128]{1,0:T(8,128)(2,1)} %ta.1, bf16[320,128]{1,0:T(8,128)(2,1)} %bitcast.8, bf16[16,128]{1,0:T(8,128)(2,1)} %qa.1, bf16[16,320]{1,0:T(8,128)(2,1)} %qg.1, s32[16]{0:T(128)} %qof_in.1, s32[16]{0:T(128)} %cnt_in.1, bf16[4,8,128,128]{3,2,1,0:T(8,128)(2,1)} %bitcast.5, ...), custom_call_target="tpu_custom_call" | custom-call | tf_op jit(solution)/shard_map/pallas_call | solution.py:544
  118.7 0.0 copy-start
  118.8 0.7 copy-done
  119.4 0.7 copy.10
  120.1 1.7 %copy.12 = f32[256,320]{0,1:T(8,128)} copy(f32[256,320]{0,1:T(8,128)} %bitcast.7) | data formatting | bytes 655360
Async XLA Ops:
  118.7 0.7 copy-start

commit v5 on v4

--- a/solution.py
+++ b/solution.py
@@ -24,7 +24,7 @@
 QR = 16
 AR = TOK + QR
 AY = 80
-GY = 240
+GY = 160
 
 
 def mod(value, size):
@@ -144,7 +144,7 @@
         return act.at[hh, z, pl.ds(lo, n), :]
 
     def g_y(hh, part):
-        lo, n = ((0, GY), (0, 128), (128, GY - 128))[0 if part is None else part + 1]
+        lo, n = ((0, GY), (0, 80), (80, GY - 80))[0 if part is None else part + 1]
         return gbuf.at[hh, z, pl.ds(lo, n), :]
 
     def act_col(hh, part):
@@ -356,27 +356,32 @@
     def held(pos):
         return (pos % 4) // 2 == k
 
-    def r_ring(hop):
+    def r_ring(hop, half):
+        if hop < 4 or half == 0:
+            pos = mod(z - hop + 1, 8)
+            send(ra_slot(pos, half), ra_slot(pos, half), rr_s.at[0, half, hop - 1], rr_r.at[0, half, hop - 1],
+                 up, held(pos))
+        if hop < 4 or half == 1:
+            pos = mod(z + hop - 1, 8)
+            send(ra_slot(pos, half), ra_slot(pos, half), rr_s.at[1, half, hop - 1], rr_r.at[1, half, hop - 1],
+                 down, held(pos))
+
+    def r_got(hop, half):
+        if hop < 4 or half == 0:
+            pos = mod(z - hop, 8)
+            arrived(ra_slot(pos, half), rr_r.at[0, half, hop - 1], held(pos))
+        if hop < 4 or half == 1:
+            pos = mod(z + hop, 8)
+            arrived(ra_slot(pos, half), rr_r.at[1, half, hop - 1], held(pos))
+
+    def r_step(hop):
         for half in range(2):
-            if hop < 4 or half == 0:
-                pos = mod(z - hop + 1, 8)
-                send(ra_slot(pos, half), ra_slot(pos, half), rr_s.at[0, half, hop - 1], rr_r.at[0, half, hop - 1],
-                     up, held(pos))
-            if hop < 4 or half == 1:
-                pos = mod(z + hop - 1, 8)
-                send(ra_slot(pos, half), ra_slot(pos, half), rr_s.at[1, half, hop - 1], rr_r.at[1, half, hop - 1],
-                     down, held(pos))
-
-    def r_got(hop):
-        for half in range(2):
-            if hop < 4 or half == 0:
-                pos = mod(z - hop, 8)
-                arrived(ra_slot(pos, half), rr_r.at[0, half, hop - 1], held(pos))
-            if hop < 4 or half == 1:
-                pos = mod(z + hop, 8)
-                arrived(ra_slot(pos, half), rr_r.at[1, half, hop - 1], held(pos))
-
-    r_ring(1)
+            r_got(hop, half)
+            if hop < 4:
+                r_ring(hop + 1, half)
+
+    r_ring(1, 0)
+    r_ring(1, 1)
     send(raq_slot(z), raq_slot(z), rk_s.at[0], rk_r.at[0], up, held(z))
     send(raq_slot(z), raq_slot(z), rk_s.at[1], rk_r.at[1], down, held(z))
 
@@ -405,16 +410,22 @@
     s_got(1, 4)
     rgb[...] = (acc[...] + s_dot(order[3])).astype(BF)
 
-    def rg_slot(s):
-        return rg.at[:, pl.ds(pl.multiple_of(s * 128, 128), 128)]
-
-    for b in range(8):
-        send(rgb, rg_slot(shard), ag_s.at[b], ag_r.at[chip], device(b % 4, b // 4, k, h, z), chip != b)
-    send(rgb, rg_slot(shard), fw_s.at[chip], fw_r.at[chip], core)
-    own_rg = local(rgb, rg_slot(shard), loc.at[4])
-
-    r_got(1)
-    r_ring(2)
+    def rg_at(xx, ll, part=None, kk=k):
+        lanes = pl.ds(pl.multiple_of(((ll * 4 + xx) * 2 + kk) * 128, 128), 128)
+        if part is None:
+            return rg.at[:, lanes]
+        return rg.at[pl.ds(part * 160, 160), lanes]
+
+    def rg_pass(xx, ll, i, src=None):
+        send(rg_at(xx, ll) if src is None else src, rg_at(xx, ll), fw_s.at[i], fw_r.at[i], core)
+
+    send(rgb, rg_at(x, l), ag_s.at[0], ag_r.at[0], beside)
+    send(rgb, rg_at(x, l), ag_s.at[1], ag_r.at[1], right)
+    send(rgb, rg_at(x, l), ag_s.at[2], ag_r.at[2], left)
+    rg_pass(x, l, 0, rgb)
+    own_rg = local(rgb, rg_at(x, l), loc.at[4])
+
+    r_step(1)
     pos = mod(z - 1, 8)
     arrived(raq_slot(pos), rk_r.at[0], held(pos))
     send(raq_slot(pos), raq_slot(pos), rk_s.at[2], rk_r.at[2], up, held(pos))
@@ -436,19 +447,36 @@
     for b in range(8):
         send(qpb.at[chip], qpb.at[chip], rq_s.at[b], rq_r.at[chip], device(b % 4, b // 4, k, h, z), chip != b)
 
-    r_got(2)
-    r_ring(3)
-    for b in range(8):
-        arrived(rg_slot(2 * b + k), ag_r.at[b], chip != b)
-        send(rg_slot(2 * b + k), rg_slot(2 * b + k), fw_s.at[b], fw_r.at[b], core, chip != b)
-    r_got(3)
-    r_ring(4)
+    arrived(rg_at(x, 1 - l), ag_r.at[0])
+    send(rg_at(x, 1 - l), rg_at(x, 1 - l), ag_s.at[3], ag_r.at[3], right)
+    send(rg_at(x, 1 - l), rg_at(x, 1 - l), ag_s.at[4], ag_r.at[4], left)
+    rg_pass(x, 1 - l, 1)
+    arrived(rg_at(xm, l), ag_r.at[1])
+    send(rg_at(xm, l, 0), rg_at(xm, l, 0), ag_s.at[5], ag_r.at[5], right)
+    rg_pass(xm, l, 2)
+    arrived(rg_at(xp, l), ag_r.at[2])
+    send(rg_at(xp, l, 1), rg_at(xp, l, 1), ag_s.at[6], ag_r.at[6], left)
+    rg_pass(xp, l, 3)
+    r_step(2)
+    arrived(rg_at(xm, 1 - l), ag_r.at[3])
+    send(rg_at(xm, 1 - l, 0), rg_at(xm, 1 - l, 0), ag_s.at[7], ag_r.at[7], right)
+    rg_pass(xm, 1 - l, 4)
+    arrived(rg_at(xp, 1 - l), ag_r.at[4])
+    send(rg_at(xp, 1 - l, 1), rg_at(xp, 1 - l, 1), ag_s.at[8], ag_r.at[8], left)
+    rg_pass(xp, 1 - l, 5)
+    r_step(3)
+    arrived(rg_at(xo, l, 0), ag_r.at[5])
+    arrived(rg_at(xo, l, 1), ag_r.at[6])
+    rg_pass(xo, l, 6)
+    arrived(rg_at(xo, 1 - l, 0), ag_r.at[7])
+    arrived(rg_at(xo, 1 - l, 1), ag_r.at[8])
+    rg_pass(xo, 1 - l, 7)
     pos = mod(z - 2, 8)
     arrived(raq_slot(pos), rk_r.at[2], held(pos))
     own_rg.wait()
-    for b in range(8):
-        arrived(rg_slot(2 * b + 1 - k), fw_r.at[b])
-    r_got(4)
+    for i, (xx, ll) in enumerate(e_of):
+        arrived(rg_at(xx, ll, None, 1 - k), fw_r.at[i])
+    r_step(4)
 
     tokens = 0
     for s in range(16):
@@ -536,7 +564,7 @@
     counts_of = [
         (4,), (4,), (2, 4), (2, 4), (8,), (8,), (9,), (9,), (4,), (4,),
         (8,), (8,), (8,), (8,), (4,), (4,), (4,), (4,),
-        (2, 2, 4), (2, 2, 4), (11,), (8,), (8,), (8,), (8,), (8,), (8,), (8,),
+        (2, 2, 4), (2, 2, 4), (11,), (8,), (8,), (8,), (9,), (9,), (8,), (8,),
         (), (), (4,), (4,), (8,), (8,), (2, 2, 4), (2, 2, 4), (3,), (3,),
         (16,), (16,), (4,), (4,), (8,), (8,), (5,),
     ]

time: 122 us -> 117 us (0.959)
  the two profiles are of different devices: /device:TPU:14 before, /device:TPU:8 now
where the time goes in v5:
time: 117 us
  Pallas kernels  113 us (97%)
  local copies, waits for them, and re-layouts  3.03 us (3%)
    pallas_call x1, Pallas kernels, per_device(): pl.pallas_call(kernel, out_shape=(jax.ShapeDtypeStruct((8, 128), F32), ja...  113 us
    unnamed x4, local copies, waits for them, and re-layouts  3.03 us

profile of v5, /device:TPU:8, one launch (start us, length us, event | category | flops | bytes accessed | tf_op | source)
XLA Modules:
  0.0 116.7 jit_solution(12795348252102860715)
XLA Ops:
  0.6 113.0 %shard_map.95 = (f32[8,128]{1,0:T(8,128)}, f32[320,256]{1,0:T(8,128)}) custom-call(bf16[128,128]{1,0:T(8,128)(2,1)} %ta.1, bf16[320,128]{1,0:T(8,128)(2,1)} %bitcast.8, bf16[16,128]{1,0:T(8,128)(2,1)} %qa.1, bf16[16,320]{1,0:T(8,128)(2,1)} %qg.1, s32[16]{0:T(128)} %qof_in.1, s32[16]{0:T(128)} %cnt_in.1, bf16[4,8,128,128]{3,2,1,0:T(8,128)(2,1)} %bitcast.5, ...), custom_call_target="tpu_custom_call" | custom-call | tf_op jit(solution)/shard_map/pallas_call | solution.py:572
  113.6 0.0 copy-start
  113.6 0.7 copy-done
  114.3 0.7 copy.10
  115.0 1.7 %copy.12 = f32[256,320]{0,1:T(8,128)} copy(f32[256,320]{0,1:T(8,128)} %bitcast.7) | data formatting | bytes 655360
Async XLA Ops:
  113.6 0.7 copy-start
